TPU v7x, 32 devices: a whole 2x2x4 slice. The times are simulated.
32 devices in a mesh: expert: 8 (over y, x, core), fsdp: 4 (over z).
Axes of the slice: x: 2, y: 2, z: 4, core: 2. Of those that a mesh axis runs over, the one named last changes fastest.
Arguments:
- inputs: bfloat16 [12288, 2048], P(('expert', 'fsdp')), may hold values from -6 to 6
- query_weight: bfloat16 [2048, 2048], P('fsdp'), may hold values from -0.125 to 0.125
- key_weight: bfloat16 [2048, 2048], P('fsdp'), may hold values from -0.125 to 0.125
- value_weight: bfloat16 [2048, 2048], P('fsdp'), may hold values from -0.125 to 0.125
- output_weight: bfloat16 [2048, 2048], P('fsdp'), may hold values from -4 to 4
- router_weight: bfloat16 [2048, 64], P('fsdp'), may hold values from -0.0625 to 0.0625
- first_gain: bfloat16 [2048], P('fsdp'), may hold values from 0.5 to 1.5
- query_gain: bfloat16 [2048], P('fsdp'), may hold values from 0.25 to 1.75
- key_gain: bfloat16 [2048], P('fsdp'), may hold values from 0.25 to 1.75
- second_gain: bfloat16 [2048], P('fsdp'), may hold values from 0.5 to 1.5
- gate_weight: bfloat16 [128, 2048, 512], P(('expert', 'fsdp')), may hold values from -0.125 to 0.125
- up_weight: bfloat16 [128, 2048, 512], P(('expert', 'fsdp')), may hold values from -0.125 to 0.125
- down_weight: bfloat16 [128, 512, 2048], P(('expert', 'fsdp')), may hold values from -6 to 6
- routes: int32 [12288, 8], P(('expert', 'fsdp')), may hold values from 0 to 63, all different within a row; in each aligned block of 384 rows (0 to 383, 384 to 767, ...) at most 56 rows name the same one
- lengths: int32 [8, 2], P('expert'), may hold values from 192 to 1344, as said below
- dealing: int32 [12288], P('expert'), may hold values from 0 to 1535, as said below
- cotangent: bfloat16 [12288, 2048], P(('expert', 'fsdp')), may hold values from -6 to 6
Outputs:
- block_output: bfloat16 [12288, 2048], P(('expert', 'fsdp'))
- input_gradient: bfloat16 [12288, 2048], P(('expert', 'fsdp'))
- query_gradient: float32 [2048, 2048], P('fsdp')
- key_gradient: float32 [2048, 2048], P('fsdp')
- value_gradient: float32 [2048, 2048], P('fsdp')
- output_gradient: float32 [2048, 2048], P('fsdp')
- router_gradient: float32 [2048, 64], P('fsdp')
- first_gain_gradient: float32 [2048], P('fsdp')
- query_gain_gradient: float32 [2048], P('fsdp')
- key_gain_gradient: float32 [2048], P('fsdp')
- second_gain_gradient: float32 [2048], P('fsdp')
- gate_gradient: float32 [128, 2048, 512], P(('expert', 'fsdp'))
- up_gradient: float32 [128, 2048, 512], P(('expert', 'fsdp'))
- down_gradient: float32 [128, 512, 2048], P(('expert', 'fsdp'))
Inputs may be any that keep to these rules, and one draw needn't show every extreme that they name: `routes`: in each aligned block of 384 rows (the rows of one device) no expert is named by more than 56 rows, and in some block one is named by exactly 56. `lengths`: each row sums to 1536: one entry, the shorter sequence, is 192 to 384, the other is the rest. `dealing`: within each group of 1536 rows, every place from 0 to 1535 once.
All inputs are finite; a program needn't handle non-finite values.
Results may differ from a plain program's by a relative error of at most 0.025.
Values may be sent and summed in bfloat16 or wider, within the bound.
A program may use at most 576 MiB of HBM per device.

v0:
```python
import functools

import jax
import jax.numpy as jnp
from jax import lax
from jax.experimental import pallas as pl
from jax.experimental.pallas import tpu as pltpu
from jax.sharding import PartitionSpec as P

HEADS = 16
CAP = 56
EPSILON = 1e-05
THETA = 10000.0
MASKED = -1e30
LOG2E = 1.4426950408889634
BF = jnp.bfloat16
F32 = jnp.float32
MESH = pl.DeviceIdType.MESH
MIB = 1 << 20
CHUNKS = 2


def dot(a, b):
    return jnp.dot(a, b, preferred_element_type=F32)


def dot_nt(a, b):
    return lax.dot_general(a, b, (((1,), (1,)), ((), ())), preferred_element_type=F32)


def dot_tn(a, b):
    return lax.dot_general(a, b, (((0,), (0,)), ((), ())), preferred_element_type=F32)


def contract(spec, *operands):
    return jnp.einsum(spec, *operands, preferred_element_type=F32)


def shape_of(dims, dtype):
    return jax.ShapeDtypeStruct(dims, dtype)


def cost(flops, moved):
    return pl.CostEstimate(flops=int(flops) // 64, bytes_accessed=int(moved) // 64, transcendentals=0)


def params(mib, **kwargs):
    return pltpu.CompilerParams(vmem_limit_bytes=mib * MIB, **kwargs)


def places(lengths_row, stream):
    seq_ends = jnp.cumsum(lengths_row)
    before = (seq_ends[None, :] <= stream[:, None]).astype(jnp.int32)
    offset = jnp.sum(before * lengths_row[None, :], axis=1)
    return offset, stream - offset


def angles(positions, head_width):
    exponent = jnp.arange(0, head_width, 2).astype(F32) / head_width
    phases = positions.astype(F32)[:, None] * (THETA ** (-exponent))[None, :]
    return jnp.cos(phases), jnp.sin(phases)


def gather_kernel(
    planes, line, pieces, x_ref, c_ref, small_ref, sent_ref,
    x_all, c_all, small_all, columns_ref, swapped_ref,
    x_send, x_recv, s_send, s_recv, z_send, z_recv, p_send, p_recv, own_sem,
):
    e, f = lax.axis_index("expert"), lax.axis_index("fsdp")
    barrier = pltpu.get_barrier_semaphore()
    for d in range(1, line):
        pl.semaphore_signal(
            barrier, inc=1, device_id={"fsdp": lax.rem(f + d, line)}, device_id_type=MESH
        )
    for d in range(1, planes):
        pl.semaphore_signal(
            barrier, inc=1, device_id={"expert": lax.rem(e + d, planes)}, device_id_type=MESH
        )
    pl.semaphore_wait(barrier, line + planes - 2)
    rows = x_ref.shape[0]
    part = rows // pieces
    small_rows = small_ref.shape[0]

    swaps, smalls = [], []
    for d in range(1, line):
        to = lax.rem(f + d, line)
        swaps.append(pltpu.make_async_remote_copy(
            src_ref=sent_ref.at[to], dst_ref=swapped_ref.at[f],
            send_sem=z_send.at[d - 1], recv_sem=z_recv.at[d - 1],
            device_id={"fsdp": to}, device_id_type=MESH,
        ))
        smalls.append(pltpu.make_async_remote_copy(
            src_ref=small_ref, dst_ref=small_all.at[pl.ds(f * small_rows, small_rows)],
            send_sem=s_send.at[d - 1], recv_sem=s_recv.at[d - 1],
            device_id={"fsdp": to}, device_id_type=MESH,
        ))
    for copy in swaps:
        copy.start()

    def hop(direction, step, c):
        own_ref, all_ref = (x_ref, x_all) if c < pieces else (c_ref, c_all)
        origin = f - direction * step
        place = pl.ds(origin * rows + c % pieces * part, part)
        cut = pl.ds(0, all_ref.shape[1])
        source = own_ref.at[pl.ds(c % pieces * part, part), cut] if step == 0 else all_ref.at[place]
        side = 0 if direction == 1 else 1
        return pltpu.make_async_remote_copy(
            src_ref=source, dst_ref=all_ref.at[place],
            send_sem=x_send.at[side, step, c], recv_sem=x_recv.at[side, step, c],
            device_id={"fsdp": f + direction}, device_id_type=MESH,
        )

    def sends(direction, step):
        origin, to = f - direction * step, f + direction
        return (origin >= 0) & (origin < line) & (to >= 0) & (to < line)

    def receives(direction, step):
        origin = f - direction * (step + 1)
        return (origin >= 0) & (origin < line)

    for direction in (1, -1):
        @pl.when(sends(direction, 0))
        def _(direction=direction):
            for c in range(2 * pieces):
                hop(direction, 0, c).start()

    for copy in smalls:
        copy.start()
    locals_ = [
        pltpu.make_async_copy(x_ref, x_all.at[pl.ds(f * rows, rows)], own_sem.at[0]),
        pltpu.make_async_copy(
            c_ref.at[:, pl.ds(0, c_all.shape[1])], c_all.at[pl.ds(f * rows, rows)], own_sem.at[4]
        ),
        pltpu.make_async_copy(
            small_ref, small_all.at[pl.ds(f * small_rows, small_rows)], own_sem.at[1]
        ),
        pltpu.make_async_copy(sent_ref.at[f], swapped_ref.at[f], own_sem.at[2]),
    ]
    for copy in locals_:
        copy.start()
    for copy in swaps:
        copy.wait_recv()
    locals_[3].wait()
    spread = []
    for d in range(1, planes):
        spread.append(pltpu.make_async_remote_copy(
            src_ref=swapped_ref, dst_ref=columns_ref.at[:, e],
            send_sem=p_send.at[d - 1], recv_sem=p_recv.at[d - 1],
            device_id={"expert": lax.rem(e + d, planes)}, device_id_type=MESH,
        ))
        spread[-1].start()
    own = pltpu.make_async_copy(swapped_ref, columns_ref.at[:, e], own_sem.at[3])
    own.start()

    for step in range(line - 1):
        for c in range(2 * pieces):
            for direction in (1, -1):
                @pl.when(receives(direction, step))
                def _(direction=direction, step=step, c=c):
                    origin = f - direction * (step + 1)
                    all_ref = x_all if c < pieces else c_all
                    place = pl.ds(origin * rows + c % pieces * part, part)
                    side = 0 if direction == 1 else 1
                    pltpu.make_async_remote_copy(
                        src_ref=all_ref.at[place], dst_ref=all_ref.at[place],
                        send_sem=x_send.at[side, step, c], recv_sem=x_recv.at[side, step, c],
                        device_id={"fsdp": f - direction}, device_id_type=MESH,
                    ).wait_recv()
                if step < line - 2:
                    @pl.when(sends(direction, step + 1))
                    def _(direction=direction, step=step, c=c):
                        hop(direction, step + 1, c).start()
    for step in range(line - 1):
        for direction in (1, -1):
            @pl.when(sends(direction, step))
            def _(direction=direction, step=step):
                for c in range(2 * pieces):
                    hop(direction, step, c).wait_send()
    for copy in swaps:
        copy.wait_send()
    for copy in smalls + spread:
        copy.wait()
    for copy in locals_[:3] + [own]:
        copy.wait()


def gather_start(block, half, small, sent, planes, line):
    rows, width = block.shape
    pieces = 4
    anywhere = pl.BlockSpec(memory_space=pl.ANY)
    sems = pltpu.SemaphoreType.DMA
    return pl.pallas_call(
        functools.partial(gather_kernel, planes, line, pieces),
        out_shape=(
            shape_of((line * rows, width), BF),
            shape_of((line * rows, half.shape[1] // 2), BF),
            shape_of((line * small.shape[0], small.shape[1]), BF),
            shape_of((line, planes) + sent.shape[1:], BF),
            shape_of(sent.shape, BF),
        ),
        in_specs=[anywhere] * 4,
        out_specs=[anywhere] * 5,
        scratch_shapes=[
            sems((2, line - 1, 2 * pieces)), sems((2, line - 1, 2 * pieces)),
            sems((line - 1,)), sems((line - 1,)), sems((line - 1,)), sems((line - 1,)),
            sems((planes - 1,)), sems((planes - 1,)), sems((5,)),
        ],
        compiler_params=pltpu.CompilerParams(collective_id=0, has_side_effects=True),
        name="gather_start",
    )(block, half, small, sent)


def line_steps(line, pieces, lag, p_ref, o_ref, right_in, left_in, send_sem, recv_sem):
    f = lax.axis_index("fsdp")
    last = line - 1
    part = p_ref.shape[0] // pieces

    def greet():
        barrier = pltpu.get_barrier_semaphore()

        @pl.when(f > 0)
        def _():
            pl.semaphore_signal(barrier, inc=1, device_id={"fsdp": f - 1}, device_id_type=MESH)

        @pl.when(f < last)
        def _():
            pl.semaphore_signal(barrier, inc=1, device_id={"fsdp": f + 1}, device_id_type=MESH)

    neighbours = jnp.where((f > 0) & (f < last), 2, 1)

    def copy(side, source, c):
        buffer = right_in if side == 0 else left_in
        place = pl.ds(c * part, part)
        return pltpu.make_async_remote_copy(
            src_ref=(p_ref if source else buffer).at[place], dst_ref=buffer.at[place],
            send_sem=send_sem.at[side, c], recv_sem=recv_sem.at[side, c],
            device_id={"fsdp": f + 1 if side == 0 else f - 1}, device_id_type=MESH,
        )

    def enter():
        for side in range(2):
            @pl.when(f == (0 if side == 0 else last))
            def _(side=side):
                def one(c, carry):
                    copy(side, True, c).start()
                    return carry

                lax.fori_loop(0, pieces, one, 0)

    def arrive(side, c):
        place = pl.ds(pl.multiple_of(c * part, part), part)
        buffer = right_in if side == 0 else left_in
        origin, end = (0, last) if side == 0 else (last, 0)
        leads = (2 * f <= last) if side == 0 else (2 * f > last)

        @pl.when(f == origin)
        def _():
            o_ref[place, :] = p_ref[place, :].astype(F32)

        @pl.when(f != origin)
        def _():
            copy(side, False, c).wait_recv()
            came = buffer[place, :].astype(F32)

            @pl.when(f != end)
            def _():
                buffer[place, :] = (came + p_ref[place, :].astype(F32)).astype(BF)
                copy(side, False, c).start()

            @pl.when(leads)
            def _():
                o_ref[place, :] = came + p_ref[place, :].astype(F32)

            @pl.when(jnp.logical_not(leads))
            def _():
                o_ref[place, :] += came

    def body(s, carry):
        for side in range(2):
            c = s - lag * (f if side == 0 else last - f)

            @pl.when((c >= 0) & (c < pieces))
            def _(side=side, c=c):
                arrive(side, c)

        return carry

    def drain():
        def one(c, carry):
            @pl.when(f < last)
            def _():
                copy(0, True, c).wait_send()

            @pl.when(f > 0)
            def _():
                copy(1, True, c).wait_send()

            return carry

        lax.fori_loop(0, pieces, one, 0)

    return greet, neighbours, enter, body, drain, pieces + lag * last


def line_sum_kernel(line, pieces, lag, p_ref, o_ref, right_in, left_in, send_sem, recv_sem):
    greet, neighbours, enter, body, drain, total = line_steps(
        line, pieces, lag, p_ref, o_ref, right_in, left_in, send_sem, recv_sem
    )
    greet()
    pl.semaphore_wait(pltpu.get_barrier_semaphore(), neighbours)
    enter()
    lax.fori_loop(0, total, body, 0)
    drain()


def line_scratch(rows, width, pieces):
    return [
        pltpu.VMEM((rows, width), BF),
        pltpu.VMEM((rows, width), BF),
        pltpu.SemaphoreType.DMA((2, pieces)),
        pltpu.SemaphoreType.DMA((2, pieces)),
    ]


def line_sum(part, line, height=32, lag=2):
    rows, width = part.shape
    pieces = rows // height
    return pl.pallas_call(
        functools.partial(line_sum_kernel, line, pieces, lag),
        out_shape=shape_of((rows, width), F32),
        in_specs=[pl.BlockSpec(memory_space=pltpu.VMEM)],
        out_specs=pl.BlockSpec(memory_space=pltpu.VMEM),
        scratch_shapes=line_scratch(rows, width, pieces),
        compiler_params=params(48, collective_id=1, has_side_effects=True),
        cost_estimate=cost(0, 260 * MIB),
        name="line_sum",
    )(part)


def line_swap_kernel(
    planes, line, pieces, lag, p_ref, rows_ref, o_ref, swapped_ref,
    right_in, left_in, send_sem, recv_sem, w_send, w_recv, own_sem,
):
    e = lax.axis_index("expert")
    greet, neighbours, enter, body, drain, total = line_steps(
        line, pieces, lag, p_ref, o_ref, right_in, left_in, send_sem, recv_sem
    )
    greet()
    barrier = pltpu.get_barrier_semaphore()
    for d in range(1, planes):
        pl.semaphore_signal(
            barrier, inc=1, device_id={"expert": lax.rem(e + d, planes)}, device_id_type=MESH
        )
    pl.semaphore_wait(barrier, neighbours + planes - 1)
    enter()
    swaps = []
    for d in range(1, planes):
        to = lax.rem(e + d, planes)
        swaps.append(pltpu.make_async_remote_copy(
            src_ref=rows_ref.at[to], dst_ref=swapped_ref.at[e],
            send_sem=w_send.at[d - 1], recv_sem=w_recv.at[d - 1],
            device_id={"expert": to}, device_id_type=MESH,
        ))
    own = pltpu.make_async_copy(rows_ref.at[e], swapped_ref.at[e], own_sem.at[0])
    for copy in swaps + [own]:
        copy.start()
    lax.fori_loop(0, total, body, 0)
    drain()
    for copy in swaps + [own]:
        copy.wait()


def line_swap(part, rows_sent, line, identity, height=32, lag=2):
    rows, width = part.shape
    planes = rows_sent.shape[0]
    pieces = rows // height
    sems = pltpu.SemaphoreType.DMA
    vmem, anywhere = pl.BlockSpec(memory_space=pltpu.VMEM), pl.BlockSpec(memory_space=pl.ANY)
    return pl.pallas_call(
        functools.partial(line_swap_kernel, planes, line, pieces, lag),
        out_shape=(shape_of((rows, width), F32), shape_of(rows_sent.shape, BF)),
        in_specs=[vmem, anywhere],
        out_specs=(vmem, anywhere),
        scratch_shapes=line_scratch(rows, width, pieces)
        + [sems((planes - 1,)), sems((planes - 1,)), sems((1,))],
        compiler_params=params(48, collective_id=identity, has_side_effects=True),
        cost_estimate=cost(0, 300 * MIB),
        name="line_swap",
    )(part, rows_sent)


def finish_kernel(
    planes, line, height, lag, p_ref, a_ref, b_ref, x_ref, gain_ref, slope_ref, gains_ref,
    o_ref, a_out, b_out, gains_out,
    right_in, left_in, a_own, a_half, a_in, a_sum, a_cols, b_own, b_half, b_in, b_sum, gain_part, gain_in, gain_own, gain_all,
    z_send, z_recv, h_send, h_recv, r_send, r_recv, s_send, s_recv, g_send, g_recv,
    w_send, w_recv, n_send, n_recv, m_send, m_recv, own_sem, slope_own,
):
    e, f = lax.axis_index("expert"), lax.axis_index("fsdp")
    chips, last = planes // 2, line - 1
    c, k = e // 2, e % 2
    mate = e + 1 - 2 * k
    barrier = pltpu.get_barrier_semaphore()

    def greet(**device):
        pl.semaphore_signal(barrier, inc=1, device_id=device, device_id_type=MESH)

    for d in range(1, planes):
        greet(expert=lax.rem(e + d, planes))
    for d in range(1, line):
        greet(fsdp=lax.rem(f + d, line))
    pl.semaphore_wait(barrier, planes - 1 + last)

    rows = p_ref.shape[0] // line
    pieces = rows // height
    ahead = 4

    def remote(source, target, send, recv, **device):
        return pltpu.make_async_remote_copy(
            src_ref=source, dst_ref=target, send_sem=send, recv_sem=recv,
            device_id=device, device_id_type=MESH,
        )

    lanes_a = a_ref.shape[-1]
    cut = lanes_a // 128 * 9 // 13 * 128
    spans = (pl.ds(0, cut), pl.ds(cut, lanes_a - cut))

    to_mate = [
        remote(
            a_ref.at[:, :, 1 - k, :, span], a_half.at[:, :, :, span], h_send.at[i], h_recv.at[i],
            expert=mate,
        )
        for i, span in enumerate(spans)
    ]
    to_mate.append(remote(b_ref.at[:, 1 - k], b_half, h_send.at[2], h_recv.at[2], expert=mate))
    own_half = [
        pltpu.make_async_copy(a_ref.at[:, :, k], a_own, own_sem.at[0]),
        pltpu.make_async_copy(b_ref.at[:, k], b_own, own_sem.at[1]),
    ]
    slope_load = pltpu.make_async_copy(
        slope_ref.at[pl.ds(pl.multiple_of(f * rows, rows), rows)], slope_own, own_sem.at[4]
    )
    for copy in to_mate + own_half + [slope_load]:
        copy.start()

    def place_of(side, s):
        target = last - s // pieces if side == 0 else s // pieces
        return target, pl.ds(pl.multiple_of(target * rows + lax.rem(s, pieces) * height, height), height)

    def copy_line(side, source, s):
        buffer = right_in if side == 0 else left_in
        place = place_of(side, s)[1]
        return remote(
            (p_ref if source else buffer).at[place], buffer.at[place],
            z_send.at[side, s], z_recv.at[side, s], fsdp=f + 1 if side == 0 else f - 1,
        )

    def begin(side, s):
        @pl.when(s >= ahead)
        def _():
            copy_line(side, True, s - ahead).wait_send()

        copy_line(side, True, s).start()

    def arrive(side, s):
        buffer = right_in if side == 0 else left_in
        target, place = place_of(side, s)
        copy_line(side, False, s).wait_recv()

        @pl.when(target != f)
        def _():
            buffer[place, :] = (buffer[place, :].astype(F32) + p_ref[place, :].astype(F32)).astype(BF)
            copy_line(side, False, s).start()

    def body(s, carry):
        right = s - lag * f
        left = s - lag * (last - f)

        @pl.when((f == 0) & (s < last * pieces))
        def _():
            begin(0, s)

        @pl.when((f == last) & (s < last * pieces))
        def _():
            begin(1, s)

        @pl.when((f > 0) & (right >= 0) & (right < (last - f + 1) * pieces))
        def _():
            arrive(0, right)

        @pl.when((f < last) & (left >= 0) & (left < (f + 1) * pieces))
        def _():
            arrive(1, left)

        return carry

    total = last * pieces + lag * last
    shares, swaps, spread = [], [], []
    sent = []

    def add_pairs():
        for copy in own_half:
            copy.wait()
        for copy in to_mate:
            copy.wait_recv()

        def one(i, carry):
            for j in range(chips):
                a_own[i, j] = (a_own[i, j].astype(F32) + a_half[i, j].astype(F32)).astype(BF)
            return carry

        lax.fori_loop(0, line, one, 0)
        for j in range(chips):
            b_own[j] = (b_own[j].astype(F32) + b_half[j].astype(F32)).astype(BF)

    def share(which):
        span = spans[which]
        mine = []
        for d in range(1, chips):
            to = lax.rem(c + d, chips)
            mine.append(remote(
                a_own.at[:, to, :, span], a_in.at[d - 1, :, :, span],
                r_send.at[which, d - 1], r_recv.at[which, d - 1], expert=to * 2 + k,
            ))
            if which:
                mine.append(remote(
                    b_own.at[to], b_in.at[d - 1], r_send.at[2, d - 1], r_recv.at[2, d - 1],
                    expert=to * 2 + k,
                ))
        for copy in mine:
            copy.start()
        shares.append(mine)

    def swap(which):
        span = spans[which]

        def one(i, carry):
            summed = a_own[i, c, :, span].astype(F32)
            for d in range(1, chips):
                summed = summed + a_in[d - 1, i, :, span].astype(F32)
            a_sum[i, :, span] = summed.astype(BF)
            return carry

        lax.fori_loop(0, line, one, 0)
        if which:
            summed = b_own[c].astype(F32)
            for d in range(1, chips):
                summed = summed + b_in[d - 1].astype(F32)
            b_sum[...] = summed.astype(BF)
        mine = []
        for d in range(1, line):
            to = lax.rem(f + d, line)
            mine.append(remote(
                a_sum.at[to, :, span], a_cols.at[f, :, span],
                s_send.at[which, d - 1], s_recv.at[which, d - 1], fsdp=to,
            ))
        for copy in mine:
            copy.start()
        a_cols[f, :, span] = a_sum[f, :, span]
        swaps.append(mine)

    def spread_out(which):
        span = spans[which]
        for copy in swaps[which]:
            copy.wait_recv()
        mine = []
        for d in range(chips):
            to = lax.rem(c + d, chips) * 2 + k if d else mate
            pair = [remote(
                a_cols.at[:, :, span], a_out.at[:, e, :, span],
                g_send.at[which, d], g_recv.at[which, d], expert=to,
            )]
            if which:
                pair.append(remote(
                    b_sum, b_out.at[e], g_send.at[2, d], g_recv.at[2, d], expert=to
                ))
            for copy in pair:
                copy.start()
            mine.append(pair)
        spread.append(mine)

    def pass_on(which):
        span = spans[which]
        for d in range(1, chips):
            for copy in spread[which][d]:
                copy.wait_recv()
            source = lax.rem(c + chips - d, chips) * 2 + k
            place = a_out.at[:, source, :, span]
            pair = [remote(
                place, place, w_send.at[which, d - 1], w_recv.at[which, d - 1], expert=mate
            )]
            if which:
                place = b_out.at[source]
                pair.append(remote(
                    place, place, w_send.at[2, d - 1], w_recv.at[2, d - 1], expert=mate
                ))
            for copy in pair:
                copy.start()
            sent.extend(pair)

    stops = [total // 10, total * 3 // 10, total // 2, total * 3 // 5, total * 3 // 4, total]
    lax.fori_loop(0, stops[0], body, 0)
    add_pairs()
    share(0)
    lax.fori_loop(stops[0], stops[1], body, 0)
    for copy in shares[0]:
        copy.wait_recv()
    share(1)
    swap(0)
    lax.fori_loop(stops[1], stops[2], body, 0)
    spread_out(0)
    lax.fori_loop(stops[2], stops[3], body, 0)
    for copy in shares[1]:
        copy.wait_recv()
    swap(1)
    lax.fori_loop(stops[3], stops[4], body, 0)
    spread_out(1)
    lax.fori_loop(stops[4], stops[5], body, 0)
    own_out = [
        pltpu.make_async_copy(a_cols, a_out.at[:, e], own_sem.at[2]),
        pltpu.make_async_copy(b_sum, b_out.at[e], own_sem.at[3]),
    ]
    for copy in own_out:
        copy.start()
    pass_on(0)

    gain = gain_ref[...]
    width = gain.shape[1]
    gain_part[...] = jnp.zeros_like(gain_part)
    slope_load.wait()

    def tile(i, carry):
        place = pl.ds(pl.multiple_of(i * height, height), height)
        mine = pl.ds(pl.multiple_of(f * rows + i * height, height), height)
        right = jnp.where(f > 0, right_in[mine, :].astype(F32), 0.0)
        left = jnp.where(f < last, left_in[mine, :].astype(F32), 0.0)
        slope = p_ref[mine, :].astype(F32) + right + left
        x = x_ref[place, :].astype(F32)
        scale = lax.rsqrt(jnp.mean(x * x, axis=-1, keepdims=True) + EPSILON)
        gain_part[0:1, :] += jnp.sum(slope * x * scale, axis=0, keepdims=True)
        slope = slope * gain
        along = jnp.sum(slope * x, axis=-1, keepdims=True) / width
        part = scale * slope - x * (scale * scale * scale * along)
        o_ref[place, :] = (slope_own[place, :] + part).astype(BF)
        return carry

    lax.fori_loop(0, pieces, tile, 0)

    lanes = gains_ref.shape[1]

    def share_of(which):
        return gain_part.at[:, pl.ds(pl.multiple_of(which * lanes, lanes), lanes)]

    to_shards = []
    for d in range(1, line):
        to = lax.rem(f + d, line)
        to_shards.append(remote(
            share_of(to), gain_in.at[d - 1], n_send.at[d - 1], n_recv.at[d - 1], fsdp=to
        ))
    for copy in to_shards:
        copy.start()
    for copy in to_shards:
        copy.wait_recv()
    summed = share_of(f)[...] + gains_ref[...]
    for d in range(1, line):
        summed = summed + gain_in[d - 1]
    gain_own[...] = summed
    to_plane = []
    for d in range(1, planes):
        to_plane.append(remote(
            gain_own, gain_all.at[d - 1], m_send.at[d - 1], m_recv.at[d - 1],
            expert=lax.rem(e + d, planes),
        ))
    for copy in to_plane:
        copy.start()

    pass_on(1)
    for copy in to_plane:
        copy.wait_recv()
    total_gain = gain_own[...]
    for d in range(1, planes):
        total_gain = total_gain + gain_all[d - 1]
    gains_out[...] = total_gain
    for mine in spread:
        for copy in mine[0]:
            copy.wait_recv()
    for copy in sent + own_out:
        copy.wait()
    for mine in spread:
        for copy in sum(mine, []):
            copy.wait_send()
    for copy in to_shards + to_plane + to_mate + sum(shares + swaps, []):
        copy.wait_send()

    def drain(side, start, stop):
        def one(s, carry):
            copy_line(side, True, s).wait_send()
            return carry

        lax.fori_loop(start, stop, one, 0)

    for side, origin in ((0, 0), (1, last)):
        count = ((last - f) if side == 0 else f) * pieces

        @pl.when(f == origin)
        def _(side=side):
            drain(side, last * pieces - ahead, last * pieces)

        @pl.when(f != origin)
        def _(side=side, count=count):
            drain(side, 0, count)


def finish(part, a, b, block, gain, slope, gains, planes, line, height=32, lag=2):
    group, width = part.shape
    tokens = group // line
    chips, last = planes // 2, line - 1
    items = last * (tokens // height)
    rows, lanes = a.shape[2:]
    share = gains.shape[1]
    vmem = pl.BlockSpec(memory_space=pltpu.VMEM)
    anywhere = pl.BlockSpec(memory_space=pl.ANY)
    sems = pltpu.SemaphoreType.DMA
    return pl.pallas_call(
        functools.partial(finish_kernel, planes, line, height, lag),
        out_shape=(
            shape_of((tokens, width), BF), shape_of(a.shape, BF), shape_of(b.shape, BF),
            shape_of(gains.shape, F32),
        ),
        in_specs=[vmem, anywhere, anywhere, vmem, vmem, anywhere, vmem],
        out_specs=(vmem, anywhere, anywhere, vmem),
        scratch_shapes=[
            pltpu.VMEM((group, width), BF), pltpu.VMEM((group, width), BF),
            pltpu.VMEM((line, chips, rows, lanes), BF), pltpu.VMEM((line, chips, rows, lanes), BF),
            pltpu.VMEM((chips - 1, line, rows, lanes), BF),
            pltpu.VMEM((line, rows, lanes), BF), pltpu.VMEM((line, rows, lanes), BF),
            pltpu.VMEM((chips, rows, width), BF), pltpu.VMEM((chips, rows, width), BF),
            pltpu.VMEM((chips - 1, rows, width), BF), pltpu.VMEM((rows, width), BF),
            pltpu.VMEM((8, width), F32), pltpu.VMEM((last, 8, share), F32),
            pltpu.VMEM((8, share), F32), pltpu.VMEM((planes - 1, 8, share), F32),
            sems((2, items)), sems((2, items)), sems((3,)), sems((3,)),
            sems((3, chips - 1)), sems((3, chips - 1)), sems((2, last)), sems((2, last)),
            sems((3, chips)), sems((3, chips)), sems((3, chips - 1)), sems((3, chips - 1)),
            sems((last,)), sems((last,)), sems((planes - 1,)), sems((planes - 1,)),
            sems((5,)), pltpu.VMEM((tokens, width), F32),
        ],
        compiler_params=params(60, collective_id=2, has_side_effects=True),
        cost_estimate=cost(0, 400 * MIB),
        name="finish",
    )(
        part, a.reshape(line, chips, 2, rows, lanes), b.reshape(chips, 2, rows, width), block, gain,
        slope, gains,
    )


def swap_plane(rows):
    return lax.all_to_all(rows, "expert", split_axis=0, concat_axis=0, tiled=True)


def small_line_sum(array, line):
    total = array
    for d in range(1, line):
        total = total + lax.ppermute(array, "fsdp", [(i, (i + d) % line) for i in range(line)])
    return total


def as_row(column, second):
    lane = lax.broadcasted_iota(jnp.int32, (column.shape[0], 128), 1)
    return jnp.where(lane == 0, column, second).T[:2, :]


def as_column(row):
    return jnp.broadcast_to(row, (128, row.shape[1])).T


def project_kernel(x_ref, gain_ref, columns_ref, normed_ref, raw_ref, value_ref, squares_ref):
    x = x_ref[...].astype(F32)
    scale = lax.rsqrt(jnp.mean(x * x, axis=-1, keepdims=True) + EPSILON)
    normed = (x * scale * gain_ref[...]).astype(BF)
    normed_ref[...] = normed
    own = value_ref.shape[1]
    query = dot(normed, columns_ref[:, :own])
    key = dot(normed, columns_ref[:, own:2 * own])
    value_ref[...] = dot(normed, columns_ref[:, 2 * own:]).astype(BF)
    raw_ref[:, :own] = query
    raw_ref[:, own:] = key
    squares_ref[...] = as_row(
        jnp.sum(query * query, axis=-1, keepdims=True), jnp.sum(key * key, axis=-1, keepdims=True)
    )


def project(block, gain, columns, tile):
    group, width = block.shape
    own = columns.shape[1] // 3
    rows = lambda count: pl.BlockSpec((tile, count), lambda i: (i, 0))
    return pl.pallas_call(
        project_kernel,
        grid=(group // tile,),
        out_shape=(
            shape_of((group, width), BF), shape_of((group, 2 * own), F32),
            shape_of((group, own), BF), shape_of((2, group), F32),
        ),
        in_specs=[
            rows(width), pl.BlockSpec((1, width), lambda i: (0, 0)),
            pl.BlockSpec((width, 3 * own), lambda i: (0, 0)),
        ],
        out_specs=(rows(width), rows(2 * own), rows(own), pl.BlockSpec((2, tile), lambda i: (0, i))),
        compiler_params=params(48),
        cost_estimate=cost(6 * group * width * own, 14 * group * own),
        name="project",
    )(block, gain, columns)


def scales_of(squares_ref, width):
    scales = lax.rsqrt(squares_ref[...] / width + EPSILON)
    return [as_column(scales[i:i + 1, :]) for i in range(2)]


def turn_kernel(width, raw_ref, squares_ref, gain_ref, cos_ref, sin_ref, q_ref, k_ref):
    own = q_ref.shape[1]
    scales = scales_of(squares_ref, width)
    cosine, sine = cos_ref[...], sin_ref[...]
    for which, out in enumerate((q_ref, k_ref)):
        for j in range(0, own, 128):
            place = slice(which * own + j, which * own + j + 128)
            v = raw_ref[:, place] * scales[which] * gain_ref[:, place]
            out[:, j:j + 128] = (v * cosine + pltpu.roll(v, 64, 1) * sine).astype(BF)


def turn(raw, squares, gain, cosine, sine, width, tile):
    group, double = raw.shape
    own = double // 2
    rows = lambda count: pl.BlockSpec((tile, count), lambda i: (i, 0))
    return pl.pallas_call(
        functools.partial(turn_kernel, width),
        grid=(group // tile,),
        out_shape=(shape_of((group, own), BF),) * 2,
        in_specs=[
            rows(double), pl.BlockSpec((2, tile), lambda i: (0, i)),
            pl.BlockSpec((1, double), lambda i: (0, 0)), rows(128), rows(128),
        ],
        out_specs=(rows(own), rows(own)),
        compiler_params=params(32),
        cost_estimate=cost(20 * group * double, 8 * group * double),
        name="turn",
    )(raw, squares, gain, cosine, sine)


def turn_back_kernel(
    width, dq_ref, dk_ref, raw_ref, squares_ref, gain_ref, cos_ref, sin_ref, dots_ref, grad_ref
):
    own = dq_ref.shape[1]
    scales = scales_of(squares_ref, width)
    cosine, sine = cos_ref[...], sin_ref[...]

    @pl.when(pl.program_id(0) == 0)
    def _():
        grad_ref[...] = jnp.zeros_like(grad_ref)

    dots = []
    for which, slope in enumerate((dq_ref, dk_ref)):
        total = 0.0
        for j in range(0, own, 128):
            place = slice(which * own + j, which * own + j + 128)
            v = slope[:, j:j + 128].astype(F32)
            turned = (v * cosine - pltpu.roll(v, 64, 1) * sine) * raw_ref[:, place]
            total = total + jnp.sum(turned * gain_ref[:, place], axis=-1, keepdims=True)
            grad_ref[:, place] += jnp.sum(turned * scales[which], axis=0, keepdims=True)
        dots.append(total)
    dots_ref[...] = as_row(*dots)


def turn_back(dq, dk, raw, squares, gain, cosine, sine, width, tile):
    group, double = raw.shape
    own = double // 2
    rows = lambda count: pl.BlockSpec((tile, count), lambda i: (i, 0))
    pair = pl.BlockSpec((2, tile), lambda i: (0, i))
    flat = pl.BlockSpec((1, double), lambda i: (0, 0))
    return pl.pallas_call(
        functools.partial(turn_back_kernel, width),
        grid=(group // tile,),
        out_shape=(shape_of((2, group), F32), shape_of((1, double), F32)),
        in_specs=[rows(own), rows(own), rows(double), pair, flat, rows(128), rows(128)],
        out_specs=(pair, flat),
        compiler_params=params(32),
        cost_estimate=cost(20 * group * double, 8 * group * double),
        name="turn_back",
    )(dq, dk, raw, squares, gain, cosine, sine)


def join_kernel(
    width, dq_ref, dk_ref, dv_ref, raw_ref, squares_ref, dots_ref, gain_ref, cos_ref, sin_ref,
    columns_ref, joint_ref, part_ref,
):
    own = dq_ref.shape[1]
    scales = scales_of(squares_ref, width)
    dots = [as_column(dots_ref[i:i + 1, :]) for i in range(2)]
    cosine, sine = cos_ref[...], sin_ref[...]
    for which, slope in enumerate((dq_ref, dk_ref)):
        scale = scales[which]
        factor = scale * scale * scale * dots[which] / width
        for j in range(0, own, 128):
            place = slice(which * own + j, which * own + j + 128)
            v = slope[:, j:j + 128].astype(F32)
            turned = (v * cosine - pltpu.roll(v, 64, 1) * sine) * gain_ref[:, place]
            joint_ref[:, place] = (scale * turned - raw_ref[:, place] * factor).astype(BF)
    joint_ref[:, 2 * own:] = dv_ref[...]
    part_ref[...] = dot_nt(joint_ref[...], columns_ref[...]).astype(BF)


def join_slopes(dq, dk, dv, raw, squares, dots, gain, cosine, sine, columns, tile):
    group, double = raw.shape
    own = double // 2
    width = columns.shape[0]
    rows = lambda count: pl.BlockSpec((tile, count), lambda i: (i, 0))
    pair = pl.BlockSpec((2, tile), lambda i: (0, i))
    flat = pl.BlockSpec((1, double), lambda i: (0, 0))
    return pl.pallas_call(
        functools.partial(join_kernel, width),
        grid=(group // tile,),
        out_shape=(shape_of((group, 3 * own), BF), shape_of((group, width), BF)),
        in_specs=[
            rows(own), rows(own), rows(own), rows(double), pair, pair, flat, rows(128), rows(128),
            pl.BlockSpec((width, 3 * own), lambda i: (0, 0)),
        ],
        out_specs=(rows(3 * own), rows(width)),
        compiler_params=params(48),
        cost_estimate=cost(6 * group * width * own, 8 * group * width),
        name="join_slopes",
    )(dq, dk, dv, raw, squares, dots, gain, cosine, sine, columns)


def allowed_scores(queries, key_rows, start_ref, place_ref, key_place_ref, inv_root):
    scores = dot_nt(key_rows, queries) * (inv_root * LOG2E)
    key_place = key_place_ref[...]
    allowed = (key_place >= start_ref[...]) & (key_place <= place_ref[...])
    return jnp.where(allowed, scores, MASKED)


def attend_kernel(size, q_ref, k_ref, v_ref, start_ref, place_ref, kp_ref, o_ref, log_ref):
    for j in range(q_ref.shape[1] // size):
        at = slice(j * size, (j + 1) * size)
        scores = allowed_scores(
            q_ref[:, at], k_ref[:, at], start_ref, place_ref, kp_ref, size ** (-0.5)
        )
        highest = jnp.max(scores, axis=0, keepdims=True)
        powers = jnp.exp2(scores - highest)
        summed = jnp.sum(powers, axis=0, keepdims=True)
        blended = dot_tn(v_ref[:, at], powers.astype(BF)) / summed
        o_ref[:, at] = blended.T.astype(BF)
        log_ref[j] = highest + jnp.log2(summed)


def attend(query, key, value, start_row, place_row, place_column, heads, tile, together=2):
    group, own_width = query.shape
    size = own_width // heads
    wide = together * size
    whole = pl.BlockSpec((group, wide), lambda h, i: (0, h))
    row = pl.BlockSpec((1, tile), lambda h, i: (0, i))
    return pl.pallas_call(
        functools.partial(attend_kernel, size),
        grid=(heads // together, group // tile),
        out_shape=(shape_of((group, own_width), BF), shape_of((heads, 1, group), F32)),
        in_specs=[
            pl.BlockSpec((tile, wide), lambda h, i: (i, h)), whole, whole, row, row,
            pl.BlockSpec((group, 1), lambda h, i: (0, 0)),
        ],
        out_specs=(
            pl.BlockSpec((tile, wide), lambda h, i: (i, h)),
            pl.BlockSpec((together, 1, tile), lambda h, i: (h, 0, i)),
        ),
        compiler_params=params(58),
        cost_estimate=cost(4 * heads * group * group * size * 4, 8 * group * own_width),
        name="attend",
    )(query, key, value, start_row, place_row, place_column)


def attend_back_kernel(
    size, q_ref, k_ref, v_ref, g_ref, log_ref, start_ref, place_ref, kp_ref,
    dq_ref, dk_ref, dv_ref, dk_sum, dv_sum,
):
    i = pl.program_id(1)
    inv_root = size ** (-0.5)

    @pl.when(i == 0)
    def _():
        dk_sum[...] = jnp.zeros_like(dk_sum)
        dv_sum[...] = jnp.zeros_like(dv_sum)

    for j in range(q_ref.shape[1] // size):
        at = slice(j * size, (j + 1) * size)
        queries, key_rows, slope = q_ref[:, at], k_ref[:, at], g_ref[:, at]
        scores = allowed_scores(queries, key_rows, start_ref, place_ref, kp_ref, inv_root)
        probability = jnp.exp2(scores - log_ref[j])
        prob_slope = dot_nt(v_ref[:, at], slope)
        product = probability * prob_slope
        row_dot = jnp.sum(product, axis=0, keepdims=True)
        score_slope = (product - probability * row_dot).astype(BF)
        dq_ref[:, at] = (dot_tn(key_rows, score_slope) * inv_root).T.astype(BF)
        dk_sum[:, at] += dot(score_slope, queries) * inv_root
        dv_sum[:, at] += dot(probability.astype(BF), slope)

    @pl.when(i == pl.num_programs(1) - 1)
    def _():
        dk_ref[...] = dk_sum[...].astype(BF)
        dv_ref[...] = dv_sum[...].astype(BF)


def attend_back(
    query, key, value, slope, log_total, start_row, place_row, place_column, heads, tile, together=2
):
    group, own_width = query.shape
    size = own_width // heads
    wide = together * size
    whole = pl.BlockSpec((group, wide), lambda h, i: (0, h))
    row = pl.BlockSpec((1, tile), lambda h, i: (0, i))
    tiled = pl.BlockSpec((tile, wide), lambda h, i: (i, h))
    return pl.pallas_call(
        functools.partial(attend_back_kernel, size),
        grid=(heads // together, group // tile),
        out_shape=(shape_of((group, own_width), BF),) * 3,
        in_specs=[
            tiled, whole, whole, tiled, pl.BlockSpec((together, 1, tile), lambda h, i: (h, 0, i)),
            row, row, pl.BlockSpec((group, 1), lambda h, i: (0, 0)),
        ],
        out_specs=(tiled, whole, whole),
        scratch_shapes=[pltpu.VMEM((group, wide), F32)] * 2,
        compiler_params=params(60),
        cost_estimate=cost(10 * heads * group * group * size * 3, 16 * group * own_width),
        name="attend_back",
    )(query, key, value, slope, log_total, start_row, place_row, place_column)


def hide_kernel(x_ref, attended_ref, gain_ref, kept_ref, hidden_ref, normed_ref):
    hidden = x_ref[...].astype(F32) + attended_ref[...]
    hidden_ref[...] = hidden
    scale = lax.rsqrt(jnp.mean(hidden * hidden, axis=-1, keepdims=True) + EPSILON)
    normed_ref[...] = (hidden * scale * gain_ref[...]).astype(BF)


def hide(block, attended, gain, offset, tile, kept):
    count, width = attended.shape
    rows = pl.BlockSpec((tile, width), lambda i: (i, 0))
    placed = pl.BlockSpec((tile, width), lambda i: (i + offset // tile, 0))
    return pl.pallas_call(
        hide_kernel,
        grid=(count // tile,),
        out_shape=(shape_of(block.shape, F32), shape_of((count, width), BF)),
        in_specs=[
            placed, rows, pl.BlockSpec((1, width), lambda i: (0, 0)),
            pl.BlockSpec(memory_space=pl.ANY),
        ],
        out_specs=(placed, rows),
        input_output_aliases={3: 0} if offset else {},
        compiler_params=params(48),
        cost_estimate=cost(8 * count * width, 12 * count * width),
        name="hide",
    )(block, attended, gain, kept)


def hide_back_kernel(
    slope_ref, hidden_ref, ca_ref, cb_ref, gain_ref, weight_ref, kept0, kept1, kept2,
    total_ref, low_ref, blend_ref, grad_ref,
):
    slope, hidden = slope_ref[...].astype(F32), hidden_ref[...]
    scale = lax.rsqrt(jnp.mean(hidden * hidden, axis=-1, keepdims=True) + EPSILON)
    part = jnp.sum(slope * hidden * scale, axis=0, keepdims=True)

    @pl.when(pl.program_id(0) == 0)
    def _():
        grad_ref[...] = part

    @pl.when(pl.program_id(0) > 0)
    def _():
        grad_ref[...] += part

    slope = slope * gain_ref[...]
    along = jnp.sum(slope * hidden, axis=-1, keepdims=True) / hidden.shape[1]
    incoming = jnp.concatenate([ca_ref[...], cb_ref[...]], axis=1).astype(F32)
    total = incoming + (
        scale * slope - hidden * (scale * scale * scale * along)
    )
    total_ref[...] = total
    low = total.astype(BF)
    low_ref[...] = low
    blend_ref[...] = dot_nt(low, weight_ref[...]).astype(BF)


def hide_back(slope, hidden, incoming, gain, weight, offset, tile, kept):
    count, width = slope.shape
    group = hidden.shape[0]
    own = weight.shape[0]
    flat = pl.BlockSpec((1, width), lambda i: (0, 0))

    def placed(size):
        return pl.BlockSpec((tile, size), lambda i: (i + offset // tile, 0))

    return pl.pallas_call(
        hide_back_kernel,
        grid=(count // tile,),
        out_shape=(
            shape_of((group, width), F32), shape_of((group, width), BF),
            shape_of((group, own), BF), shape_of((1, width), F32),
        ),
        in_specs=[
            pl.BlockSpec((tile, width), lambda i: (i, 0)), placed(width), placed(width // 2),
            placed(width // 2), flat, pl.BlockSpec((own, width), lambda i: (0, 0)),
        ]
        + [pl.BlockSpec(memory_space=pl.ANY)] * 3,
        out_specs=(placed(width), placed(width), placed(own), flat),
        input_output_aliases={6: 0, 7: 1, 8: 2} if offset else {},
        compiler_params=params(56),
        cost_estimate=cost(2 * count * width * own, 18 * count * width),
        name="hide_back",
    )(slope, hidden, *incoming, gain, weight, *kept)


def widen_kernel(own, a_ref, b_ref, query_ref, key_ref, value_ref, out_ref, router_ref):
    line, _, _, rows, _ = a_ref.shape
    for f in range(line):
        for which, o_ref in enumerate((query_ref, key_ref, value_ref)):
            o_ref[:, f * own:(f + 1) * own] = a_ref[
                f, 0, 0, :, which * own:(which + 1) * own
            ].astype(F32)
    out_ref[...] = b_ref[0, 0].astype(F32)
    routing = a_ref[0, 0, 0, :, 3 * own:].astype(F32)
    for f in range(1, line):
        routing = routing + a_ref[f, 0, 0, :, 3 * own:].astype(F32)
    router_ref[...] = routing


def widen(a, b, own):
    line, chips, _, rows, lanes = a.shape
    width = b.shape[-1]
    extra = lanes - 3 * own
    count = 2 * chips * rows
    full, part = shape_of((count, width), F32), shape_of((count, extra), F32)
    wide = pl.BlockSpec((rows, width), lambda i: (i, 0))
    return pl.pallas_call(
        functools.partial(widen_kernel, own),
        grid=(2 * chips,),
        out_shape=(full,) * 4 + (part,),
        in_specs=[
            pl.BlockSpec((line, 1, 1, rows, lanes), lambda i: (0, i // 2, i % 2, 0, 0)),
            pl.BlockSpec((1, 1, rows, width), lambda i: (i // 2, i % 2, 0, 0)),
        ],
        out_specs=(wide,) * 4 + (pl.BlockSpec((rows, extra), lambda i: (i, 0)),),
        compiler_params=params(32),
        cost_estimate=cost(8 * count * width, 24 * count * width),
        name="widen",
    )(a, b)


def joint_grad_kernel(normed_ref, joint_ref, router_ref, o_ref):
    size = joint_ref.shape[1]
    o_ref[:, :size] = dot(normed_ref[...].T, joint_ref[...]).astype(BF)
    o_ref[:, size:] = router_ref[...]


def joint_grad(normed, joint, router):
    group, width = normed.shape
    size, extra = joint.shape[1], router.shape[1]
    tile = 512
    return pl.pallas_call(
        joint_grad_kernel,
        grid=(width // tile,),
        out_shape=shape_of((width, size + extra), BF),
        in_specs=[
            pl.BlockSpec((group, tile), lambda j: (0, j)),
            pl.BlockSpec((group, size), lambda j: (0, 0)),
            pl.BlockSpec((tile, extra), lambda j: (j, 0)),
        ],
        out_specs=pl.BlockSpec((tile, size + extra), lambda j: (j, 0)),
        compiler_params=params(56),
        cost_estimate=cost(2 * group * width * size, 6 * group * width),
        name="joint_grad",
    )(normed, joint, router)


def dispatch_kernel(slots, code_ref, rows_ref, o_ref, select):
    pairs = code_ref.shape[1]

    @pl.when(pl.program_id(1) == 0)
    def _():
        for i in range(pairs):
            row = code_ref[0, i:i + 1, :]
            slot = lax.broadcasted_iota(jnp.int32, (slots, row.shape[1]), 0).astype(F32)
            select[i * slots:(i + 1) * slots, :] = (slot == row).astype(BF)

    chosen = dot(select[...], rows_ref[...]).astype(BF)
    o_ref[...] = chosen.reshape(o_ref.shape)


def dispatch(codes, rows, planes, local, slots):
    chunks, pairs, count = codes.shape
    width = rows.shape[1]
    tile = 512
    return pl.pallas_call(
        functools.partial(dispatch_kernel, slots),
        grid=(chunks, width // tile),
        out_shape=shape_of((planes, local, chunks * slots, width), BF),
        in_specs=[
            pl.BlockSpec((1, pairs, count), lambda k, j: (k, 0, 0)),
            pl.BlockSpec((count, tile), lambda k, j: (k, j)),
        ],
        out_specs=pl.BlockSpec((planes, local, slots, tile), lambda k, j: (0, 0, k, j)),
        scratch_shapes=[pltpu.VMEM((pairs * slots, count), BF)],
        compiler_params=params(48),
        cost_estimate=cost(2 * pairs * slots * chunks * count * width, 4 * pairs * slots * width),
        name="dispatch",
    )(codes, rows)


def combine_kernel(slots, code_ref, rows_ref, o_ref, select):
    pairs = code_ref.shape[2]

    @pl.when(pl.program_id(1) == 0)
    def _():
        total = pairs * slots
        lane = lax.broadcasted_iota(jnp.int32, (pairs, total), 1)
        start = lax.broadcasted_iota(jnp.int32, (pairs, total), 0) * slots
        within = (lane >= start) & (lane < start + slots)
        spread = dot(code_ref[0], within.astype(BF))
        slot = jnp.sum(jnp.where(within, lane - start, 0), axis=0, keepdims=True)
        select[...] = (spread == slot.astype(F32)).astype(BF)

    rows = rows_ref[...].reshape(pairs * slots, rows_ref.shape[-1])
    o_ref[...] = dot(select[...], rows).astype(BF)


def combine(codes, rows, slots):
    planes, local, _, width = rows.shape
    chunks, count, pairs = codes.shape
    tile = 512
    return pl.pallas_call(
        functools.partial(combine_kernel, slots),
        grid=(chunks, width // tile),
        out_shape=shape_of((chunks * count, width), BF),
        in_specs=[
            pl.BlockSpec((1, count, pairs), lambda k, j: (k, 0, 0)),
            pl.BlockSpec((planes, local, slots, tile), lambda k, j: (0, 0, k, j)),
        ],
        out_specs=pl.BlockSpec((count, tile), lambda k, j: (k, j)),
        scratch_shapes=[pltpu.VMEM((count, pairs * slots), BF)],
        compiler_params=params(56),
        cost_estimate=cost(2 * pairs * slots * chunks * count * width, 4 * pairs * slots * width),
        name="combine",
    )(codes, rows)


def expert_kernel(
    halves, x_ref, ca_ref, cb_ref, gate_ref, up_ref, down_ref, router_ref, named_ref, kept_ref,
    weighted_ref, slope_ref, act_ref, gslope_ref, uslope_ref, logit_ref,
):
    width = x_ref.shape[-1]
    x = x_ref[...].reshape(-1, width)
    c = jnp.concatenate(
        [ref[...].reshape(-1, width // 2) for ref in (ca_ref, cb_ref)], axis=1
    ).astype(F32)
    router = router_ref[...]
    logits = dot(x, router)
    powers = jnp.exp(logits - jnp.max(logits, axis=-1, keepdims=True))
    chance = powers / jnp.sum(powers, axis=-1, keepdims=True)
    named = named_ref[0]
    gating = jnp.sum(chance * named, axis=-1, keepdims=True)
    joined = None
    kept = []
    for h in range(halves):
        gate_pre = dot(x, gate_ref[h])
        up_pre = dot(x, up_ref[h])
        squashed = jax.nn.sigmoid(gate_pre)
        swished = gate_pre * squashed
        activation = swished * up_pre
        act_ref[h] = (gating * activation).astype(BF)
        part = dot(activation.astype(BF), down_ref[h])
        joined = part if joined is None else joined + part
        kept.append((up_pre * squashed * (1.0 + gate_pre * (1.0 - squashed)), swished))
    gating_slope = jnp.sum(c * joined, axis=-1, keepdims=True)
    weighted_ref[...] = (gating * joined).astype(BF).reshape(weighted_ref.shape)
    unit_slope = (gating * c).astype(BF)
    logit_slope = (gating_slope * gating * (named - chance)).astype(BF)
    logit_ref[...] = logit_slope[None]
    slope = dot_nt(logit_slope, router)
    for h in range(halves):
        activation_slope = dot_nt(unit_slope, down_ref[h])
        gate_slope = (activation_slope * kept[h][0]).astype(BF)
        up_slope = (activation_slope * kept[h][1]).astype(BF)
        gslope_ref[h] = gate_slope
        uslope_ref[h] = up_slope
        slope = slope + dot_nt(gate_slope, gate_ref[h]) + dot_nt(up_slope, up_ref[h])
    slope_ref[...] = slope.astype(BF).reshape(slope_ref.shape)


def experts(x, cs, at, gates, ups, downs, router, named, halves, kept):
    planes, local, slots, width = x.shape
    hidden = gates.shape[-1]
    sources = max(1, 448 // slots)
    tile = sources * slots
    steps = planes // sources
    count = planes * slots
    expert_total = router.shape[1]
    units = local * halves
    row_spec = pl.BlockSpec((sources, 1, slots, width), lambda n, t: (t, n, 0, 0))
    half_spec = pl.BlockSpec((sources, 1, slots, width // 2), lambda n, t: (t, n, at, 0))
    unit_spec = pl.BlockSpec((halves, tile, hidden), lambda n, t: (n, t, 0))
    once = pl.Buffered(1)
    wide = pl.BlockSpec((halves, width, hidden), lambda n, t: (n, 0, 0), pipeline_mode=once)
    tall = pl.BlockSpec((halves, hidden, width), lambda n, t: (n, 0, 0), pipeline_mode=once)
    return pl.pallas_call(
        functools.partial(expert_kernel, halves),
        grid=(local, steps),
        out_shape=(
            shape_of((planes, local, CHUNKS * slots, width), BF), shape_of(x.shape, BF),
            shape_of((units, count, hidden), BF), shape_of((units, count, hidden), BF),
            shape_of((units, count, hidden), BF), shape_of((local, count, expert_total), BF),
        ),
        in_specs=[
            row_spec, half_spec, half_spec, wide, wide, tall,
            pl.BlockSpec((width, expert_total), lambda n, t: (0, 0)),
            pl.BlockSpec((1, 1, expert_total), lambda n, t: (n, 0, 0)),
            pl.BlockSpec(memory_space=pl.ANY),
        ],
        out_specs=(
            pl.BlockSpec((sources, 1, slots, width), lambda n, t: (t, n, at, 0)), row_spec, unit_spec, unit_spec, unit_spec,
            pl.BlockSpec((1, tile, expert_total), lambda n, t: (n, t, 0)),
        ),
        input_output_aliases={8: 0} if at else {},
        compiler_params=params(62),
        cost_estimate=cost(12 * units * count * hidden * width, 10 * local * count * width),
        name="experts",
    )(x, *cs, gates, ups, downs, router, named, kept)


def wide_grad_kernel(x0_ref, x1_ref, g0_ref, g1_ref, u0_ref, u1_ref, dg_ref, du_ref):
    tile = x0_ref.shape[-1]
    x0 = x0_ref[...].reshape(-1, tile).T
    x1 = x1_ref[...].reshape(-1, tile).T
    dg_ref[0] = dot(x0, g0_ref[0]) + dot(x1, g1_ref[0])
    du_ref[0] = dot(x0, u0_ref[0]) + dot(x1, u1_ref[0])


def wide_grad(xs, gslopes, uslopes, halves):
    planes, local, slots, width = xs[0].shape
    units, count, hidden = gslopes[0].shape
    tile = 1024 if planes * slots <= 1024 else 512
    x_spec = pl.BlockSpec((planes, 1, slots, tile), lambda u, j: (0, u // halves, 0, j))
    s_spec = pl.BlockSpec((1, count, hidden), lambda u, j: (u, 0, 0))
    o_spec = pl.BlockSpec((1, tile, hidden), lambda u, j: (u, j, 0))
    out = shape_of((units, width, hidden), F32)
    return pl.pallas_call(
        wide_grad_kernel,
        grid=(units, width // tile),
        out_shape=(out, out),
        in_specs=[x_spec] * 2 + [s_spec] * 4,
        out_specs=(o_spec, o_spec),
        compiler_params=params(60),
        cost_estimate=cost(8 * units * count * hidden * width, 8 * units * hidden * width),
        name="wide_grad",
    )(*xs, *gslopes, *uslopes)


def down_grad_kernel(a0_ref, a1_ref, ca_ref, cb_ref, d_ref):
    tile, slots = ca_ref.shape[-1], ca_ref.shape[2] // 2

    def part(c_ref):
        d_ref[0] = dot(a0_ref[0].T, c_ref[:, :, :slots].reshape(-1, tile)) + dot(
            a1_ref[0].T, c_ref[:, :, slots:].reshape(-1, tile)
        )

    first = pl.program_id(1) < pl.num_programs(1) // 2
    pl.when(first)(lambda: part(ca_ref))
    pl.when(jnp.logical_not(first))(lambda: part(cb_ref))


def down_grad(acts, cs, halves):
    planes, local, double, half = cs[0].shape
    units, count, hidden = acts[0].shape
    tile = half if planes * double <= 2048 else 512
    steps = half // tile
    a_spec = pl.BlockSpec((1, count, hidden), lambda u, j: (u, 0, 0))
    shape = (planes, 1, double, tile)
    return pl.pallas_call(
        down_grad_kernel,
        grid=(units, 2 * steps),
        out_shape=shape_of((units, hidden, 2 * half), F32),
        in_specs=[
            a_spec, a_spec,
            pl.BlockSpec(shape, lambda u, j: (0, u // halves, 0, jnp.minimum(j, steps - 1))),
            pl.BlockSpec(shape, lambda u, j: (0, u // halves, 0, jnp.maximum(j - steps, 0))),
        ],
        out_specs=pl.BlockSpec((1, hidden, tile), lambda u, j: (u, 0, j)),
        compiler_params=params(60),
        cost_estimate=cost(8 * units * count * hidden * half, 8 * units * hidden * half),
        name="down_grad",
    )(*acts, *cs)


def per_device(
    inputs,
    query_weight,
    key_weight,
    value_weight,
    output_weight,
    router_weight,
    first_gain,
    query_gain,
    key_gain,
    second_gain,
    gate_weight,
    up_weight,
    down_weight,
    routes,
    lengths,
    dealing,
    cotangent,
):
    planes, line = lax.axis_size("expert"), lax.axis_size("fsdp")
    plane_at, line_at = lax.axis_index("expert"), lax.axis_index("fsdp")
    tokens, width = inputs.shape
    group = line * tokens
    own_heads = HEADS // line
    head_size = width // HEADS
    own_width = own_heads * head_size
    weight_rows = query_weight.shape[0]
    slice_rows = weight_rows // planes
    units = gate_weight.shape[0]
    local = max(1, units // 2)
    halves = units // local
    expert_count = router_weight.shape[1]
    blocks = line // CHUNKS
    chunk_rows = blocks * tokens
    slots = blocks * CAP

    def own_slice(weight):
        return lax.dynamic_slice_in_dim(weight, plane_at * slice_rows, slice_rows, 0)

    sent = jnp.stack([own_slice(w) for w in (query_weight, key_weight, value_weight)], axis=1)
    sent = jnp.moveaxis(sent.reshape(slice_rows, 3, line, own_width), 2, 0)
    sent = sent.reshape(line, slice_rows, 3 * own_width)
    top_count = routes.shape[1]
    packed = [router_weight, first_gain, second_gain, routes.astype(BF)]
    sizes = [array.size for array in packed]
    fill = -sum(sizes) % (16 * 128)
    small = jnp.concatenate([array.reshape(-1) for array in packed] + [jnp.zeros((fill,), BF)])
    block_in, first_half, small_all, columns, _ = gather_start(
        inputs, cotangent, small.reshape(-1, 128), sent, planes, line
    )
    columns = columns.reshape(width, 3 * own_width)
    small_all = small_all.reshape(line, -1)
    ends = [sum(sizes[:i]) for i in range(5)]
    full_router, gain_first, gain_second, routes_all = (
        small_all[:, ends[i]:ends[i + 1]] for i in range(4)
    )
    full_router = full_router.reshape(width, expert_count)
    gain_first, gain_second = (g.reshape(width).astype(F32) for g in (gain_first, gain_second))
    routes_all = routes_all.reshape(line, tokens, top_count).astype(jnp.int32)
    later, _ = lax.optimization_barrier((cotangent, block_in))
    second_half = lax.all_gather(later[:, width // 2:], "fsdp", axis=0, tiled=True)
    incoming = [first_half, second_half]

    seq_start, positions = places(lengths[0], dealing)
    start_row, place_row, place_column = seq_start[None, :], dealing[None, :], dealing[:, None]
    cosine, sine = angles(positions, head_size)
    per_plane = expert_count // planes
    first_local = (line_at * units) // 2
    member = jnp.sum(
        (routes_all[..., None] == jnp.arange(expert_count, dtype=jnp.int32)).astype(F32), axis=2
    )
    earlier = jnp.tril(jnp.ones((tokens, tokens), BF), -1)
    rank = contract("ts,bse->bte", earlier, member.astype(BF))
    rank = rank + ((jnp.arange(line) % blocks) * CAP).astype(F32)[:, None, None]
    coded = jnp.where(member > 0, rank, -1.0).reshape(line, tokens, planes, per_plane)
    coded = lax.dynamic_slice_in_dim(coded, first_local, local, 3)
    coded = coded.reshape(CHUNKS, chunk_rows, planes * local)
    by_token = coded.astype(BF)
    by_pair = jnp.swapaxes(coded, 1, 2)

    def chunk(array, k):
        return lax.slice_in_dim(array, k * chunk_rows, (k + 1) * chunk_rows)

    rows = dispatch(by_pair, incoming[0], planes, local, slots)
    normed_low, raw, value_low, squares = project(block_in, gain_first[None], columns, tokens)
    squares = small_line_sum(squares, line)
    both_gains = jnp.concatenate([query_gain, key_gain])[None].astype(F32)
    rotary = (jnp.concatenate([cosine, cosine], -1), jnp.concatenate([-sine, sine], -1))
    query_low, key_low = turn(raw, squares, both_gains, *rotary, width, tokens)
    blended, log_total = attend(
        query_low, key_low, value_low, start_row, place_row, place_column, own_heads, tokens
    )
    attention_part = dot(blended, output_weight).astype(BF)

    named = (
        (((plane_at * line + line_at) * units) // 2 + jnp.arange(local))[:, None, None]
        == jnp.arange(expert_count)
    ).astype(F32)
    attention_parts = [chunk(attention_part, k) for k in range(CHUNKS)]
    arrived_slopes = [swap_plane(rows)]
    rows = dispatch(by_pair, incoming[1], planes, local, slots)
    attended, swapped = line_swap(attention_parts[0], rows, line, 4)
    arrived_slopes.append(swapped)
    hidden, arrived = block_in, []
    for k in range(CHUNKS):
        hidden, normed = hide(block_in, attended, gain_second[None], k * chunk_rows, tokens, hidden)
        rows = dispatch(by_pair[k:k + 1], normed, planes, local, slots)
        if k + 1 < CHUNKS:
            attended, swapped = line_swap(attention_parts[k + 1], rows, line, 3)
            arrived.append(swapped)
        else:
            rows, arrived_slopes[0] = lax.optimization_barrier((rows, arrived_slopes[0]))
            arrived.append(swap_plane(rows))
    weighted = arrived_slopes[0]
    row_slopes, acts, gslopes, uslopes, logit_slopes = [], [], [], [], []
    for k in range(CHUNKS):
        results = experts(
            arrived[k], arrived_slopes, k, gate_weight, up_weight, down_weight, full_router,
            named, halves, weighted,
        )
        weighted = results[0]
        for store, result in zip((row_slopes, acts, gslopes, uslopes, logit_slopes), results[1:]):
            store.append(result)
    returned = []
    behind = arrived[-1]
    for k in range(CHUNKS):
        rows, _ = lax.optimization_barrier((row_slopes[k], behind))
        behind = swap_plane(rows)
        returned.append(behind)

    second_gain_grad = 0.0
    kept = (block_in,) * 3
    for k in range(CHUNKS):
        returned[k], _ = lax.optimization_barrier((returned[k], summed if k else row_slopes[-1]))
        part = combine(by_token[k:k + 1], returned[k], slots)
        if k:
            rows, _ = lax.optimization_barrier((weighted, returned[k]))
            mixed_rows = swap_plane(rows)
        summed = line_sum(part, line)
        *kept, gain_part = hide_back(
            summed, hidden, incoming, gain_second[None], output_weight, k * chunk_rows, tokens, kept
        )
        second_gain_grad = second_gain_grad + gain_part
    hidden_slope, attention_slope, blended_slope = kept
    slopes = attend_back(
        query_low, key_low, value_low, blended_slope, log_total, start_row,
        place_row, place_column, own_heads, tokens,
    )
    dots, gain_grads = turn_back(*slopes[:2], raw, squares, both_gains, *rotary, width, tokens)
    dots = small_line_sum(dots, line)
    mixed_rows, _ = lax.optimization_barrier((mixed_rows, gain_grads))
    mixed = combine(by_token, mixed_rows, slots)
    acts, gslopes, uslopes, logit_slopes, attention_slope, _ = lax.optimization_barrier(
        (acts, gslopes, uslopes, logit_slopes, attention_slope, mixed)
    )
    mixed = lax.psum_scatter(mixed, "fsdp", scatter_dimension=0, tiled=True)
    expert_grads = [
        *wide_grad(arrived, gslopes, uslopes, halves),
        down_grad(acts, arrived_slopes, halves),
    ]
    router_grad = sum(
        contract(
            "ensd,nesq->dq", arrived[k],
            logit_slopes[k].reshape(local, planes, slots, expert_count),
        )
        for k in range(CHUNKS)
    )
    output_grad = contract("tc,td->cd", blended, attention_slope).astype(BF)
    dots, _ = lax.optimization_barrier((dots, expert_grads))
    joint, normed_part = join_slopes(
        *slopes, raw, squares, dots, both_gains, *rotary, columns, tokens
    )
    router_lanes = -expert_count % 128
    router_pad = jnp.pad(router_grad.astype(BF), ((0, 0), (0, router_lanes)))
    joint_total = joint_grad(normed_low, joint, router_pad)
    mine = line_at * weight_rows
    second_own = lax.dynamic_slice_in_dim(second_gain_grad, mine, weight_rows, 1)
    gain_rows = jnp.concatenate(
        [
            jnp.zeros((1, weight_rows), F32), second_own, gain_grads.reshape(2, own_width),
            jnp.zeros((4, weight_rows), F32),
        ]
    )
    input_gradient, totals, output_total, gain_totals = finish(
        normed_part, joint_total.reshape(line, planes, slice_rows, -1),
        output_grad.reshape(planes, slice_rows, width), inputs, gain_first[None],
        hidden_slope, gain_rows, planes, line,
    )
    hidden_own = lax.dynamic_slice_in_dim(hidden, line_at * tokens, tokens, 0)
    block_output = (hidden_own + mixed.astype(F32)).astype(BF)
    *weight_grads, router_total = widen(
        totals.reshape(line, planes // 2, 2, slice_rows, -1),
        output_total.reshape(planes // 2, 2, slice_rows, width), own_width,
    )
    router_total = router_total[:, :expert_count]
    return (
        block_output,
        input_gradient,
        *weight_grads,
        router_total,
        gain_totals[0],
        gain_totals[2],
        gain_totals[3],
        gain_totals[1],
        *expert_grads,
    )


def solution(mesh):
    both = ("expert", "fsdp")
    rows, cube, shard, gain = P(both, None), P(both, None, None), P("fsdp", None), P("fsdp")
    return jax.shard_map(
        per_device,
        mesh=mesh,
        in_specs=(rows,)
        + (shard,) * 5
        + (gain,) * 4
        + (cube,) * 3
        + (rows, P("expert", None), P("expert"), rows),
        out_specs=(rows, rows) + (shard,) * 5 + (gain,) * 4 + (cube,) * 3,
        check_vma=False,
    )
```

profile of v0, /device:TPU:0, one launch (start us, length us, event | category | flops | bytes accessed | tf_op | source)
XLA Modules:
  0.0 1270.9 jit_solution(664554544183083350)
XLA Ops:
  15.8 189.9 %gather_start.1 = (bf16[1536,2048]{1,0:T(8,128)(2,1)}, bf16[1536,1024]{1,0:T(8,128)(2,1)}, bf16[1152,128]{1,0:T(8,128)(2,1)}, bf16[4,8,64,1536]{3,2,1,0:T(8,128)(2,1)}, bf16[4,64,1536]{2,1,0:T(8,128)(2,1)}) custom-call(bf16[384,2048]{1,0:T(8,128)(2,1)} %x_ref.3, bf16[384,2048]{1,0:T(8,128)(2,1)} %c_ref.1, bf16[288,128]{1,0:T(8,128)(2,1)} %maximum_bitcast_fusion.1.small_ref, ...), custom_call_target="tpu_custom_call" | custom-call | tf_op jit(solution)/shard_map/gather_start/pallas_call | solution.py:192
  215.6 8.9 dispatch.7
  224.4 5.0 all-to-all-start
  230.6 15.6 %project.1 = (bf16[1536,2048]{1,0:T(8,128)(2,1)}, f32[1536,1024]{1,0:T(8,128)}, bf16[1536,512]{1,0:T(8,128)(2,1)S(1)}, f32[2,1536]{1,0:T(2,128)S(1)}) custom-call(bf16[1536,2048]{1,0:T(8,128)(2,1)} %get-tuple-element.91.x_ref.kept_ref.kept0.kept1.kept2, f32[1,2048]{1,0:T(1,128)S(1)} %bitcast.70, bf16[2048,1536]{1,0:T(8,128)(2,1)} %bitcast.73), custom_call_target="tpu_custom_call" | custom-call | flops 150994944 | bytes 172032 | tf_op jit(solution)/shard_map/project/pallas_call | solution.py:796
  247.3 2.5 collective-permute-start.2
  250.9 2.8 fusion.10
  256.9 2.5 turn.1
  261.8 21.7 %attend.1 = (bf16[1536,512]{1,0:T(8,128)(2,1)}, f32[4,1,1536]{2,1,0:T(1,128)}) custom-call(bf16[1536,512]{1,0:T(8,128)(2,1)} %copy-done.13, bf16[1536,512]{1,0:T(8,128)(2,1)} %copy-done.14, bf16[1536,512]{1,0:T(8,128)(2,1)} %copy-done.12, s32[1,1536]{1,0:T(1,128)} %broadcast_in_dim.20.start_ref, s32[1,1536]{1,0:T(1,128)} %broadcast_in_dim.21.place_ref, ...), custom_call_target="tpu_custom_call" | custom-call | flops 301989888 | bytes 98304 | tf_op jit(solution)/shard_map/attend/pallas_call | solution.py:960
  283.5 5.1 convolution_convert_fusion
  288.5 2.5 fusion.19
  291.0 6.3 all-gather.2.cloned.1.call-done.rows_ref.cb_ref
  299.3 8.8 dispatch.4.rows_ref
  308.1 86.0 %line_swap.2 = (f32[768,2048]{1,0:T(8,128)}, bf16[8,2,224,1024]{3,2,1,0:T(8,128)(2,1)}) custom-call(bf16[768,2048]{1,0:T(8,128)(2,1)S(1)} %copy-done.4, bf16[8,2,224,1024]{3,2,1,0:T(8,128)(2,1)} %dispatch.4.rows_ref), custom_call_target="tpu_custom_call" | custom-call | bytes 4915200 | tf_op jit(solution)/shard_map/line_swap/pallas_call | solution.py:379
  394.1 6.3 hide.2
  400.4 8.4 dispatch.5.rows_ref
  408.7 86.2 %line_swap.3 = (f32[768,2048]{1,0:T(8,128)}, bf16[8,2,112,2048]{3,2,1,0:T(8,128)(2,1)}) custom-call(bf16[768,2048]{1,0:T(8,128)(2,1)S(1)} %get-tuple-element.225.p_ref, bf16[8,2,112,2048]{3,2,1,0:T(8,128)(2,1)} %dispatch.5.rows_ref), custom_call_target="tpu_custom_call" | custom-call | bytes 4915200 | tf_op jit(solution)/shard_map/line_swap/pallas_call | solution.py:379
  495.0 6.3 hide.3
  501.3 8.4 dispatch.6
  509.6 5.0 all-to-all-start.1
  516.5 75.9 %experts.2 = (bf16[8,2,224,2048]{3,2,1,0:T(8,128)(2,1)}, bf16[8,2,112,2048]{3,2,1,0:T(8,128)(2,1)}, bf16[4,896,512]{2,1,0:T(8,128)(2,1)}, bf16[4,896,512]{2,1,0:...) custom-call(bf16[8,2,112,2048]{3,2,1,0:T(8,128)(2,1)} %get-tuple-element.111.x_ref.x0_ref, ...), custom_call_target="tpu_custom_call" | custom-call | flops 704643072 | bytes 573440 | tf_op jit(solution)/shard_map/experts/pallas_call | solution.py:1309
  592.4 5.1 all-to-all-done.1.x_ref.x1_ref
  597.4 4.9 all-to-all-start.2
  602.4 76.4 %experts.3 = (bf16[8,2,224,2048]{3,2,1,0:T(8,128)(2,1)}, bf16[8,2,112,2048]{3,2,1,0:T(8,128)(2,1)}, bf16[4,896,512]{2,1,0:T(8,128)(2,1)}, bf16[4,896,512]{2,1,0:...) custom-call(bf16[8,2,112,2048]{3,2,1,0:T(8,128)(2,1)} %all-to-all-done.1, ...), custom_call_target="tpu_custom_call", output_to_operand_aliasing={{0}: (8, {})} | custom-call | flops 704643072 | bytes 573440 | tf_op jit(solution)/shard_map/experts/pallas_call | solution.py:1309
  678.7 6.4 all-to-all-done.2.rows_ref
  685.2 5.0 all-to-all-start.3
  691.3 9.8 combine.3.p_ref
  703.0 83.7 %line_sum.2.slope_ref = f32[768,2048]{1,0:T(8,128)} custom-call(bf16[768,2048]{1,0:T(8,128)(2,1)S(1)} %copy-done.5), custom_call_target="tpu_custom_call" | custom-call | bytes 4259840 | tf_op jit(solution)/shard_map/line_sum/pallas_call | solution.py:328
  786.7 5.6 all-to-all-start.4
  792.4 11.3 hide_back.2
  803.7 9.8 combine.4.p_ref
  815.4 83.6 %line_sum.3.slope_ref = f32[768,2048]{1,0:T(8,128)} custom-call(bf16[768,2048]{1,0:T(8,128)(2,1)S(1)} %copy-done.6), custom_call_target="tpu_custom_call" | custom-call | bytes 4259840 | tf_op jit(solution)/shard_map/line_sum/pallas_call | solution.py:328
  899.1 11.3 hide_back.3
  910.4 37.7 %attend_back.1 = (bf16[1536,512]{1,0:T(8,128)(2,1)}, bf16[1536,512]{1,0:T(8,128)(2,1)}, bf16[1536,512]{1,0:T(8,128)(2,1)}) custom-call(bf16[1536,512]{1,0:T(8,128)(2,1)} %copy-done.13, bf16[1536,512]{1,0:T(8,128)(2,1)} %copy-done.14, bf16[1536,512]{1,0:T(8,128)(2,1)} %copy-done.12, bf16[1536,512]{1,0:T(8,128)(2,1)} %get-tuple-element.124.g_ref, ...), custom_call_target="tpu_custom_call" | custom-call | flops 566231040 | bytes 196608 | tf_op jit(solution)/shard_map/attend_back/pallas_call | solution.py:1018
  948.1 2.8 copy-done.1
  953.7 5.6 turn_back.1
  959.3 17.9 %combine.5 = bf16[1536,2048]{1,0:T(8,128)(2,1)} custom-call(bf16[2,768,16]{2,1,0:T(8,128)(2,1)} %copy-done.24, bf16[8,2,224,2048]{3,2,1,0:T(8,128)(2,1)} %all-to-all-done.4.rows_ref), custom_call_target="tpu_custom_call" | custom-call | flops 176160768 | bytes 229376 | tf_op jit(solution)/shard_map/combine/pallas_call | solution.py:1235
  983.6 27.4 %down_grad.1 = f32[4,512,2048]{2,1,0:T(8,128)} custom-call(bf16[4,896,512]{2,1,0:T(8,128)(2,1)} %get-tuple-element.147.a0_ref, bf16[4,896,512]{2,1,0:T(8,128)(2,1)} %get-tuple-element.148.a1_ref, bf16[8,2,224,1024]{3,2,1,0:T(8,128)(2,1)} %all-to-all-done.ca_ref.kept_ref, bf16[8,2,224,1024]{3,2,1,0:T(8,128)(2,1)} %get-tuple-element.110.cb_ref), custom_call_target="tpu_custom_call" | custom-call | flops 234881024 | bytes 262144 | tf_op jit(solution)/shard_map/down_grad/pallas_call | solution.py:1382
  1011.0 41.1 %wide_grad.1 = (f32[4,2048,512]{2,1,0:T(8,128)}, f32[4,2048,512]{2,1,0:T(8,128)}) custom-call(bf16[8,2,112,2048]{3,2,1,0:T(8,128)(2,1)} %get-tuple-element.111.x_ref.x0_ref, bf16[8,2,112,2048]{3,2,1,0:T(8,128)(2,1)} %all-to-all-done.1.x_ref.x1_ref, bf16[4,896,512]{2,1,0:T(8,128)(2,1)} %get-tuple-element.141.g0_ref, ...), custom_call_target="tpu_custom_call" | custom-call | flops 469762048 | bytes 524288 | tf_op jit(solution)/shard_map/wide_grad/pallas_call | solution.py:1350
  1052.2 4.6 convolution_bitcast_fusion.1
  1056.8 5.4 fusion
  1062.1 2.0 copy.84
  1067.4 17.3 %join_slopes.1 = (bf16[1536,1536]{1,0:T(8,128)(2,1)}, bf16[1536,2048]{1,0:T(8,128)(2,1)}) custom-call(bf16[1536,512]{1,0:T(8,128)(2,1)S(1)} %copy-done.16, bf16[1536,512]{1,0:T(8,128)(2,1)S(1)} %copy-done.18, bf16[1536,512]{1,0:T(8,128)(2,1)} %get-tuple-element.130.dv_ref, f32[1536,1024]{1,0:T(8,128)} %get-tuple-element.94.raw_ref, ...), custom_call_target="tpu_custom_call" | custom-call | flops 150994944 | bytes 393216 | tf_op jit(solution)/shard_map/join_slopes/pallas_call | solution.py:918
  1084.7 15.2 %joint_grad.1 = bf16[2048,1664]{1,0:T(8,128)(2,1)} custom-call(bf16[1536,2048]{1,0:T(8,128)(2,1)} %get-tuple-element.151.normed_ref, bf16[1536,1536]{1,0:T(8,128)(2,1)} %get-tuple-element.152.joint_ref, bf16[2048,128]{1,0:T(8,128)(2,1)} %pad.4.router_ref), custom_call_target="tpu_custom_call" | custom-call | flops 150994944 | bytes 294912 | tf_op jit(solution)/shard_map/joint_grad/pallas_call | solution.py:1164
  1099.9 7.4 convolution_convert_fusion.1
  1107.3 138.8 %finish.1 = (bf16[384,2048]{1,0:T(8,128)(2,1)}, bf16[4,8,64,1664]{3,2,1,0:T(8,128)(2,1)}, bf16[8,64,2048]{2,1,0:T(8,128)(2,1)}, f32[8,512]{1,0:T(8,128)}) custom-call(bf16[1536,2048]{1,0:T(8,128)(2,1)} %get-tuple-element.150.p_ref, bf16[4,4,2,64,1664]{4,3,2,1,0:T(8,128)(2,1)} %bitcast.72, bf16[4,2,64,2048]{3,2,1,0:T(8,128)(2,1)} %bitcast.75, ...), custom_call_target="tpu_custom_call" | custom-call | bytes 6553600 | tf_op jit(solution)/shard_map/finish/pallas_call | solution.py:724
  1246.2 2.9 copy-done.11
  1250.7 6.4 widen.1
  1258.5 4.0 add_convert_fusion
  (156 shorter events, 52.4 us)
Async XLA Ops:
  9.3 5.8 copy-start.32
  9.3 5.8 copy-start.33
  205.7 9.9 copy-start.2
  206.9 23.5 %copy-start.26 = (bf16[4,36864]{1,0:T(4,128)(2,1)}, bf16[4,36864]{1,0:T(4,128)(2,1)S(1)}, u32[]{:S(2)}) copy-start(bf16[4,36864]{1,0:T(4,128)(2,1)S(1)} %reshape.230) | copy-start | bytes 884740
  224.4 5.1 copy-start.23
  224.4 285.2 %all-to-all-start = ((bf16[8,2,224,1024]{3,2,1,0:T(8,128)(2,1)}), bf16[8,2,224,1024]{3,2,1,0:T(8,128)(2,1)}, u32[]{:S(2)}, u32[]{:S(2)}) async-start(bf16[8,2,224,1024]{3,2,1,0:T(8,128)(2,1)} %dispatch.7), calls=%async_computation | async-start | bytes 14680064 | tf_op jit(solution)/shard_map/all_to_all | solution.py:757
  229.4 68.0 %all-gather.2.cloned.1.call-start = ((), (), s32[]{:S(2)}) async-start(), calls=%async_computation.6 | async-start | bytes 3932160 | tf_op jit(solution)/shard_map/all_gather | solution.py:1458
  230.5 15.6 %copy-start.21 = (f32[1,1,4,512]{3,1,2,0:T(1,128)}, f32[1,1,4,512]{3,1,2,0:T(1,128)S(1)}, u32[]{:S(2)}) copy-start(f32[1,1,4,512]{3,1,2,0:T(1,128)S(1)} %copy.93) | copy-start | bytes 24580
  230.5 20.1 %copy-start.34 = (bf16[512]{0:T(512)(128)(2,1)S(1)}, bf16[512]{0:T(512)(128)(2,1)}, u32[]{:S(2)}) copy-start(bf16[512]{0:T(512)(128)(2,1)} %param.25) | copy-start | bytes 3076
  230.5 20.0 %copy-start.35 = (bf16[512]{0:T(512)(128)(2,1)S(1)}, bf16[512]{0:T(512)(128)(2,1)}, u32[]{:S(2)}) copy-start(bf16[512]{0:T(512)(128)(2,1)} %param.24) | copy-start | bytes 3076
  230.5 20.1 %copy-start.36 = (s32[1,2]{1,0:T(1,128)S(1)}, s32[1,2]{1,0:T(1,128)}, u32[]{:S(2)}) copy-start(s32[1,2]{1,0:T(1,128)} %param.31) | copy-start | bytes 28
  230.5 20.2 %copy-start.30 = (s32[1536]{0:T(1024)S(1)}, s32[1536]{0:T(1024)}, u32[]{:S(2)}) copy-start(s32[1536]{0:T(1024)} %param.32) | copy-start | bytes 18436
  247.3 9.3 collective-permute-start.2
  249.8 7.1 collective-permute-start.1
  249.8 7.1 collective-permute-start
  250.8 6.2 copy-start
  254.2 5.3 copy-start.7
  254.2 5.3 copy-start.9
  256.6 238.3 %copy-start.20 = (f32[1,1,4,512]{3,1,2,0:T(1,128)}, f32[1,1,4,512]{3,1,2,0:T(1,128)S(1)}, u32[]{:S(2)}) copy-start(f32[1,1,4,512]{3,1,2,0:T(1,128)S(1)} %copy.94) | copy-start | bytes 24580
  261.8 21.7 %copy-start.22 = (bf16[512,2048]{1,0:T(8,128)(2,1)S(1)}, bf16[512,2048]{1,0:T(8,128)(2,1)}, u32[]{:S(2)}) copy-start(bf16[512,2048]{1,0:T(8,128)(2,1)} %weight_ref.3) | copy-start | bytes 6291460
  297.4 1.9 copy-start.3
  299.3 8.8 copy-start.4
  509.6 5.0 slice-start
  509.6 87.8 %all-to-all-start.1 = ((bf16[8,2,112,2048]{3,2,1,0:T(8,128)(2,1)}), bf16[8,2,112,2048]{3,2,1,0:T(8,128)(2,1)}, u32[]{:S(2)}, u32[]{:S(2)}) async-start(bf16[8,2,112,2048]{3,2,1,0:T(8,128)(2,1)} %dispatch.6), calls=%async_computation.1 | async-start | bytes 14680064 | tf_op jit(solution)/shard_map/all_to_all | solution.py:757
  597.4 87.7 %all-to-all-start.2 = ((bf16[8,2,112,2048]{3,2,1,0:T(8,128)(2,1)}), bf16[8,2,112,2048]{3,2,1,0:T(8,128)(2,1)}, u32[]{:S(2)}, u32[]{:S(2)}) async-start(bf16[8,2,112,2048]{3,2,1,0:T(8,128)(2,1)} %get-tuple-element.116), calls=%async_computation.2 | async-start | bytes 14680064 | tf_op jit(solution)/shard_map/all_to_all | solution.py:757
  685.2 5.0 copy-start.27
  685.2 101.5 %all-to-all-start.3 = ((bf16[8,2,112,2048]{3,2,1,0:T(8,128)(2,1)}), bf16[8,2,112,2048]{3,2,1,0:T(8,128)(2,1)}, u32[]{:S(2)}, u32[]{:S(2)}) async-start(bf16[8,2,112,2048]{3,2,1,0:T(8,128)(2,1)} %get-tuple-element.117), calls=%async_computation.3 | async-start | bytes 14680064 | tf_op jit(solution)/shard_map/all_to_all | solution.py:757
  690.4 10.7 copy-start.24
  701.1 1.9 copy-start.5
  786.7 172.6 %all-to-all-start.4 = ((bf16[8,2,224,2048]{3,2,1,0:T(8,128)(2,1)}), bf16[8,2,224,2048]{3,2,1,0:T(8,128)(2,1)}, u32[]{:S(2)}, u32[]{:S(2)}) async-start(bf16[8,2,224,2048]{3,2,1,0:T(8,128)(2,1)} %get-tuple-element.120), calls=%async_computation.4 | async-start | bytes 29360128 | tf_op jit(solution)/shard_map/all_to_all | solution.py:757
  792.3 466.2 %reduce-scatter.2.cloned.1.call-start = ((), (), s32[]{:S(2)}) async-start(), calls=%async_computation.7 | async-start | bytes 7864320 | tf_op jit(solution)/shard_map/reduce_scatter | solution.py:1553
  813.5 1.9 copy-start.6
  910.4 37.7 %copy-start.8 = (f32[1536,128]{1,0:T(8,128)S(1)}, f32[1536,128]{1,0:T(8,128)}, u32[]{:S(2)}) copy-start(f32[1536,128]{1,0:T(8,128)} %copy-done.7) | copy-start | bytes 2359300
  910.4 37.7 %copy-start.10 = (f32[1536,128]{1,0:T(8,128)S(1)}, f32[1536,128]{1,0:T(8,128)}, u32[]{:S(2)}) copy-start(f32[1536,128]{1,0:T(8,128)} %copy-done.9) | copy-start | bytes 2359300
  948.1 2.8 copy-start.1
  950.9 1.4 copy-start.15
  977.3 4.6 collective-permute-start.5
  977.8 4.6 collective-permute-start.4
  978.1 5.5 collective-permute-start.3
  1011.0 41.1 %copy-start.28 = (bf16[2,896,64]{2,1,0:T(8,128)(2,1)S(1)}, bf16[2,896,64]{2,1,0:T(8,128)(2,1)}, u32[]{:S(2)}) copy-start(bf16[2,896,64]{2,1,0:T(8,128)(2,1)} %get-tuple-element.153) | copy-start | bytes 688132
  1052.2 4.6 copy-start.29
  1056.8 9.3 copy-start.16
  1066.0 1.4 copy-start.18
  1084.7 15.2 %copy-start.37 = (bf16[1536,512]{1,0:T(8,128)(2,1)S(1)}, bf16[1536,512]{1,0:T(8,128)(2,1)}, u32[]{:S(2)}) copy-start(bf16[1536,512]{1,0:T(8,128)(2,1)} %get-tuple-element.99) | copy-start | bytes 4718596
  1246.1 2.9 copy-start.11
  1249.1 1.6 copy-start.19
  1250.7 7.2 copy-start.31
  1257.1 5.4 copy-start.25
  (4 other events, 4.9 us)
Sparse Core Ops, SparseCore 0:
  232.4 64.9 all-gather.1
  977.4 108.9 reduce-scatter.1
where the time goes:
time: 1280 us; the launch traced here: 1270 us
  Pallas kernels  1120 us (88%)
  local copies, waits for them, and re-layouts  49.6 us (4%)
  starting transfers between devices  30.8 us (2%)
  matrix products  23.9 us (2%)
  waiting for transfers between devices  19.8 us (2%)
  between operations  15.2 us (1%)
  other arithmetic  13.5 us (1%)
    pallas_call x1, Pallas kernels, gather_start(): pl.pallas_call(functools.partial(gather_kernel, planes, line, pieces), ou...  190 us
    pallas_call x2, Pallas kernels, line_swap(): pl.pallas_call(functools.partial(line_swap_kernel, planes, line, pieces,...  172 us
    pallas_call x2, Pallas kernels, line_sum(): pl.pallas_call(functools.partial(line_sum_kernel, line, pieces, lag), out...  167 us
    pallas_call x2, Pallas kernels, experts(): pl.pallas_call(functools.partial(expert_kernel, halves), grid=(local, ste...  152 us
    pallas_call x1, Pallas kernels, finish(): pl.pallas_call(functools.partial(finish_kernel, planes, line, height, lag...  139 us
    pallas_call x1, Pallas kernels, wide_grad(): pl.pallas_call(wide_grad_kernel, grid=(units, width // tile), out_shape=(...  41.1 us
    pallas_call x1, Pallas kernels, attend_back(): pl.pallas_call(functools.partial(attend_back_kernel, size), grid=(heads /...  37.7 us
    pallas_call x3, Pallas kernels, combine(): pl.pallas_call(functools.partial(combine_kernel, slots), grid=(chunks, wi...  37.6 us
  transfers between devices with their start and end apart: 13, of which 6 were waited for; matrix products, arithmetic and copies ran while one was open for 3% of the time, Pallas kernels for 71%

commit v1 on v0

--- a/solution.py
+++ b/solution.py
@@ -210,7 +210,7 @@
     )(block, half, small, sent)
 
 
-def line_steps(line, pieces, lag, p_ref, o_ref, right_in, left_in, send_sem, recv_sem):
+def line_steps(line, pieces, lag, p_ref, o_ref, right_in, left_in, send_sem, recv_sem, complete):
     f = lax.axis_index("fsdp")
     last = line - 1
     part = p_ref.shape[0] // pieces
@@ -274,6 +274,7 @@
             @pl.when(jnp.logical_not(leads))
             def _():
                 o_ref[place, :] += came
+                complete(place, c)
 
     def body(s, carry):
         for side in range(2):
@@ -300,17 +301,6 @@
         lax.fori_loop(0, pieces, one, 0)
 
     return greet, neighbours, enter, body, drain, pieces + lag * last
-
-
-def line_sum_kernel(line, pieces, lag, p_ref, o_ref, right_in, left_in, send_sem, recv_sem):
-    greet, neighbours, enter, body, drain, total = line_steps(
-        line, pieces, lag, p_ref, o_ref, right_in, left_in, send_sem, recv_sem
-    )
-    greet()
-    pl.semaphore_wait(pltpu.get_barrier_semaphore(), neighbours)
-    enter()
-    lax.fori_loop(0, total, body, 0)
-    drain()
 
 
 def line_scratch(rows, width, pieces):
@@ -322,28 +312,50 @@
     ]
 
 
-def line_sum(part, line, height=32, lag=2):
-    rows, width = part.shape
-    pieces = rows // height
-    return pl.pallas_call(
-        functools.partial(line_sum_kernel, line, pieces, lag),
-        out_shape=shape_of((rows, width), F32),
-        in_specs=[pl.BlockSpec(memory_space=pltpu.VMEM)],
-        out_specs=pl.BlockSpec(memory_space=pltpu.VMEM),
-        scratch_shapes=line_scratch(rows, width, pieces),
-        compiler_params=params(48, collective_id=1, has_side_effects=True),
-        cost_estimate=cost(0, 260 * MIB),
-        name="line_sum",
-    )(part)
-
-
-def line_swap_kernel(
-    planes, line, pieces, lag, p_ref, rows_ref, o_ref, swapped_ref,
-    right_in, left_in, send_sem, recv_sem, w_send, w_recv, own_sem,
+def store_pieces(pairs, sems, pieces, height):
+    def copies(c):
+        place = pl.ds(pl.multiple_of(c * height, height), height)
+        return [
+            pltpu.make_async_copy(source.at[place], target.at[place], sems.at[i, c])
+            for i, (source, target) in enumerate(pairs)
+        ]
+
+    def start(c):
+        for copy in copies(c):
+            copy.start()
+
+    def wait():
+        def one(c, carry):
+            for copy in copies(c):
+                copy.wait()
+            return carry
+
+        lax.fori_loop(0, pieces, one, 0)
+
+    return start, wait
+
+
+def hide_kernel(
+    planes, line, pieces, lag, at, p_ref, x_ref, gain_ref, rows_ref, hidden_ref, normed_ref, swapped_ref,
+    right_in, left_in, send_sem, recv_sem, w_send, w_recv, own_sem, x_own, total_own, normed_own, store_sem,
 ):
     e = lax.axis_index("expert")
+    rows = p_ref.shape[0]
+    load = pltpu.make_async_copy(x_ref.at[pl.ds(at * rows, rows)], x_own, own_sem.at[1])
+    load.start()
+    start_store, wait_stores = store_pieces(
+        [(total_own, hidden_ref), (normed_own, normed_ref)], store_sem, pieces, rows // pieces
+    )
+
+    def complete(place, c):
+        hidden = x_own[place, :].astype(F32) + total_own[place, :]
+        total_own[place, :] = hidden
+        scale = lax.rsqrt(jnp.mean(hidden * hidden, axis=-1, keepdims=True) + EPSILON)
+        normed_own[place, :] = (hidden * scale * gain_ref[...]).astype(BF)
+        start_store(c)
+
     greet, neighbours, enter, body, drain, total = line_steps(
-        line, pieces, lag, p_ref, o_ref, right_in, left_in, send_sem, recv_sem
+        line, pieces, lag, p_ref, total_own, right_in, left_in, send_sem, recv_sem, complete
     )
     greet()
     barrier = pltpu.get_barrier_semaphore()
@@ -364,33 +376,113 @@
     own = pltpu.make_async_copy(rows_ref.at[e], swapped_ref.at[e], own_sem.at[0])
     for copy in swaps + [own]:
         copy.start()
+    load.wait()
     lax.fori_loop(0, total, body, 0)
     drain()
     for copy in swaps + [own]:
         copy.wait()
-
-
-def line_swap(part, rows_sent, line, identity, height=32, lag=2):
+    wait_stores()
+
+
+def hide(part, block, gain, rows_sent, at, line, identity, height=32, lag=2):
     rows, width = part.shape
     planes = rows_sent.shape[0]
     pieces = rows // height
     sems = pltpu.SemaphoreType.DMA
-    vmem, anywhere = pl.BlockSpec(memory_space=pltpu.VMEM), pl.BlockSpec(memory_space=pl.ANY)
+    anywhere = pl.BlockSpec(memory_space=pl.ANY)
+    vmem = pl.BlockSpec(memory_space=pltpu.VMEM)
     return pl.pallas_call(
-        functools.partial(line_swap_kernel, planes, line, pieces, lag),
-        out_shape=(shape_of((rows, width), F32), shape_of(rows_sent.shape, BF)),
-        in_specs=[vmem, anywhere],
-        out_specs=(vmem, anywhere),
+        functools.partial(hide_kernel, planes, line, pieces, lag, at),
+        out_shape=(
+            shape_of((rows, width), F32), shape_of((rows, width), BF),
+            shape_of(rows_sent.shape, BF),
+        ),
+        in_specs=[vmem, anywhere, vmem, anywhere],
+        out_specs=(anywhere, anywhere, anywhere),
         scratch_shapes=line_scratch(rows, width, pieces)
-        + [sems((planes - 1,)), sems((planes - 1,)), sems((1,))],
-        compiler_params=params(48, collective_id=identity, has_side_effects=True),
+        + [
+            sems((planes - 1,)), sems((planes - 1,)), sems((2,)),
+            pltpu.VMEM((rows, width), BF), pltpu.VMEM((rows, width), F32),
+            pltpu.VMEM((rows, width), BF), sems((2, pieces)),
+        ],
+        compiler_params=params(60, collective_id=identity, has_side_effects=True),
         cost_estimate=cost(0, 300 * MIB),
-        name="line_swap",
-    )(part, rows_sent)
+        name="hide",
+    )(part, block, gain, rows_sent)
+
+
+def hide_back_kernel(
+    line, pieces, lag, at, p_ref, hidden_ref, ca_ref, cb_ref, gain_ref, total_ref, low_ref, grad_ref,
+    right_in, left_in, send_sem, recv_sem, hidden_own, ca_own, cb_own, total_own, low_own, load_sem, store_sem,
+):
+    rows = p_ref.shape[0]
+    half = ca_ref.shape[1]
+    mine = pl.ds(at * rows, rows)
+    loads = [
+        pltpu.make_async_copy(hidden_ref, hidden_own, load_sem.at[0]),
+        pltpu.make_async_copy(ca_ref.at[mine], ca_own, load_sem.at[1]),
+        pltpu.make_async_copy(cb_ref.at[mine], cb_own, load_sem.at[2]),
+    ]
+    for copy in loads:
+        copy.start()
+    start_store, wait_stores = store_pieces(
+        [(total_own, total_ref), (low_own, low_ref)], store_sem, pieces, rows // pieces
+    )
+
+    def complete(place, c):
+        slope, hidden = total_own[place, :], hidden_own[place, :]
+        scale = lax.rsqrt(jnp.mean(hidden * hidden, axis=-1, keepdims=True) + EPSILON)
+        grad_ref[...] += jnp.sum(slope * hidden * scale, axis=0, keepdims=True)
+        slope = slope * gain_ref[...]
+        along = jnp.sum(slope * hidden, axis=-1, keepdims=True) / hidden.shape[1]
+        part = scale * slope - hidden * (scale * scale * scale * along)
+        for ref, lanes in ((ca_own, slice(0, half)), (cb_own, slice(half, 2 * half))):
+            total = ref[place, :].astype(F32) + part[:, lanes]
+            total_own[place, lanes] = total
+            low_own[place, lanes] = total.astype(BF)
+        start_store(c)
+
+    greet, neighbours, enter, body, drain, total = line_steps(
+        line, pieces, lag, p_ref, total_own, right_in, left_in, send_sem, recv_sem, complete
+    )
+    greet()
+    grad_ref[...] = jnp.zeros_like(grad_ref)
+    pl.semaphore_wait(pltpu.get_barrier_semaphore(), neighbours)
+    enter()
+    for copy in loads:
+        copy.wait()
+    lax.fori_loop(0, total, body, 0)
+    drain()
+    wait_stores()
+
+
+def hide_back(part, hidden, incoming, gain, at, line, height=32, lag=2):
+    rows, width = part.shape
+    pieces = rows // height
+    sems = pltpu.SemaphoreType.DMA
+    anywhere = pl.BlockSpec(memory_space=pl.ANY)
+    vmem = pl.BlockSpec(memory_space=pltpu.VMEM)
+    return pl.pallas_call(
+        functools.partial(hide_back_kernel, line, pieces, lag, at),
+        out_shape=(
+            shape_of((rows, width), F32), shape_of((rows, width), BF), shape_of((1, width), F32),
+        ),
+        in_specs=[vmem, anywhere, anywhere, anywhere, vmem],
+        out_specs=(anywhere, anywhere, vmem),
+        scratch_shapes=line_scratch(rows, width, pieces)
+        + [
+            pltpu.VMEM((rows, width), F32), pltpu.VMEM((rows, width // 2), BF),
+            pltpu.VMEM((rows, width // 2), BF), pltpu.VMEM((rows, width), F32),
+            pltpu.VMEM((rows, width), BF), sems((3,)), sems((2, pieces)),
+        ],
+        compiler_params=params(62, collective_id=5 + at, has_side_effects=True),
+        cost_estimate=cost(0, 260 * MIB),
+        name="hide_back",
+    )(part, hidden, *incoming, gain)
 
 
 def finish_kernel(
-    planes, line, height, lag, p_ref, a_ref, b_ref, x_ref, gain_ref, slope_ref, gains_ref,
+    planes, line, height, lag, p_ref, a_ref, b_ref, x_ref, gain_ref, slope0_ref, slope1_ref, gains_ref,
     o_ref, a_out, b_out, gains_out,
     right_in, left_in, a_own, a_half, a_in, a_sum, a_cols, b_own, b_half, b_in, b_sum, gain_part, gain_in, gain_own, gain_all,
     z_send, z_recv, h_send, h_recv, r_send, r_recv, s_send, s_recv, g_send, g_recv,
@@ -437,10 +529,16 @@
         pltpu.make_async_copy(a_ref.at[:, :, k], a_own, own_sem.at[0]),
         pltpu.make_async_copy(b_ref.at[:, k], b_own, own_sem.at[1]),
     ]
-    slope_load = pltpu.make_async_copy(
-        slope_ref.at[pl.ds(pl.multiple_of(f * rows, rows), rows)], slope_own, own_sem.at[4]
-    )
-    for copy in to_mate + own_half + [slope_load]:
+    blocks = line // 2
+
+    def slope_load(which):
+        source = (slope0_ref, slope1_ref)[which]
+        place = pl.ds(pl.multiple_of((f - which * blocks) * rows, rows), rows)
+        return pltpu.make_async_copy(source.at[place], slope_own, own_sem.at[4])
+
+    pl.when(f < blocks)(lambda: slope_load(0).start())
+    pl.when(f >= blocks)(lambda: slope_load(1).start())
+    for copy in to_mate + own_half:
         copy.start()
 
     def place_of(side, s):
@@ -627,7 +725,8 @@
     gain = gain_ref[...]
     width = gain.shape[1]
     gain_part[...] = jnp.zeros_like(gain_part)
-    slope_load.wait()
+    pl.when(f < blocks)(lambda: slope_load(0).wait())
+    pl.when(f >= blocks)(lambda: slope_load(1).wait())
 
     def tile(i, carry):
         place = pl.ds(pl.multiple_of(i * height, height), height)
@@ -711,7 +810,7 @@
             drain(side, 0, count)
 
 
-def finish(part, a, b, block, gain, slope, gains, planes, line, height=32, lag=2):
+def finish(part, a, b, block, gain, slopes, gains, planes, line, height=32, lag=2):
     group, width = part.shape
     tokens = group // line
     chips, last = planes // 2, line - 1
@@ -727,7 +826,7 @@
             shape_of((tokens, width), BF), shape_of(a.shape, BF), shape_of(b.shape, BF),
             shape_of(gains.shape, F32),
         ),
-        in_specs=[vmem, anywhere, anywhere, vmem, vmem, anywhere, vmem],
+        in_specs=[vmem, anywhere, anywhere, vmem, vmem, anywhere, anywhere, vmem],
         out_specs=(vmem, anywhere, anywhere, vmem),
         scratch_shapes=[
             pltpu.VMEM((group, width), BF), pltpu.VMEM((group, width), BF),
@@ -749,7 +848,7 @@
         name="finish",
     )(
         part, a.reshape(line, chips, 2, rows, lanes), b.reshape(chips, 2, rows, width), block, gain,
-        slope, gains,
+        *slopes, gains,
     )
 
 
@@ -1029,90 +1128,6 @@
         cost_estimate=cost(10 * heads * group * group * size * 3, 16 * group * own_width),
         name="attend_back",
     )(query, key, value, slope, log_total, start_row, place_row, place_column)
-
-
-def hide_kernel(x_ref, attended_ref, gain_ref, kept_ref, hidden_ref, normed_ref):
-    hidden = x_ref[...].astype(F32) + attended_ref[...]
-    hidden_ref[...] = hidden
-    scale = lax.rsqrt(jnp.mean(hidden * hidden, axis=-1, keepdims=True) + EPSILON)
-    normed_ref[...] = (hidden * scale * gain_ref[...]).astype(BF)
-
-
-def hide(block, attended, gain, offset, tile, kept):
-    count, width = attended.shape
-    rows = pl.BlockSpec((tile, width), lambda i: (i, 0))
-    placed = pl.BlockSpec((tile, width), lambda i: (i + offset // tile, 0))
-    return pl.pallas_call(
-        hide_kernel,
-        grid=(count // tile,),
-        out_shape=(shape_of(block.shape, F32), shape_of((count, width), BF)),
-        in_specs=[
-            placed, rows, pl.BlockSpec((1, width), lambda i: (0, 0)),
-            pl.BlockSpec(memory_space=pl.ANY),
-        ],
-        out_specs=(placed, rows),
-        input_output_aliases={3: 0} if offset else {},
-        compiler_params=params(48),
-        cost_estimate=cost(8 * count * width, 12 * count * width),
-        name="hide",
-    )(block, attended, gain, kept)
-
-
-def hide_back_kernel(
-    slope_ref, hidden_ref, ca_ref, cb_ref, gain_ref, weight_ref, kept0, kept1, kept2,
-    total_ref, low_ref, blend_ref, grad_ref,
-):
-    slope, hidden = slope_ref[...].astype(F32), hidden_ref[...]
-    scale = lax.rsqrt(jnp.mean(hidden * hidden, axis=-1, keepdims=True) + EPSILON)
-    part = jnp.sum(slope * hidden * scale, axis=0, keepdims=True)
-
-    @pl.when(pl.program_id(0) == 0)
-    def _():
-        grad_ref[...] = part
-
-    @pl.when(pl.program_id(0) > 0)
-    def _():
-        grad_ref[...] += part
-
-    slope = slope * gain_ref[...]
-    along = jnp.sum(slope * hidden, axis=-1, keepdims=True) / hidden.shape[1]
-    incoming = jnp.concatenate([ca_ref[...], cb_ref[...]], axis=1).astype(F32)
-    total = incoming + (
-        scale * slope - hidden * (scale * scale * scale * along)
-    )
-    total_ref[...] = total
-    low = total.astype(BF)
-    low_ref[...] = low
-    blend_ref[...] = dot_nt(low, weight_ref[...]).astype(BF)
-
-
-def hide_back(slope, hidden, incoming, gain, weight, offset, tile, kept):
-    count, width = slope.shape
-    group = hidden.shape[0]
-    own = weight.shape[0]
-    flat = pl.BlockSpec((1, width), lambda i: (0, 0))
-
-    def placed(size):
-        return pl.BlockSpec((tile, size), lambda i: (i + offset // tile, 0))
-
-    return pl.pallas_call(
-        hide_back_kernel,
-        grid=(count // tile,),
-        out_shape=(
-            shape_of((group, width), F32), shape_of((group, width), BF),
-            shape_of((group, own), BF), shape_of((1, width), F32),
-        ),
-        in_specs=[
-            pl.BlockSpec((tile, width), lambda i: (i, 0)), placed(width), placed(width // 2),
-            placed(width // 2), flat, pl.BlockSpec((own, width), lambda i: (0, 0)),
-        ]
-        + [pl.BlockSpec(memory_space=pl.ANY)] * 3,
-        out_specs=(placed(width), placed(width), placed(own), flat),
-        input_output_aliases={6: 0, 7: 1, 8: 2} if offset else {},
-        compiler_params=params(56),
-        cost_estimate=cost(2 * count * width * own, 18 * count * width),
-        name="hide_back",
-    )(slope, hidden, *incoming, gain, weight, *kept)
 
 
 def widen_kernel(own, a_ref, b_ref, query_ref, key_ref, value_ref, out_ref, router_ref):
@@ -1331,15 +1346,18 @@
     )(x, *cs, gates, ups, downs, router, named, kept)
 
 
-def wide_grad_kernel(x0_ref, x1_ref, g0_ref, g1_ref, u0_ref, u1_ref, dg_ref, du_ref):
+def wide_grad_kernel(
+    x0_ref, x1_ref, g0_ref, g1_ref, u0_ref, u1_ref, l0_ref, l1_ref, dg_ref, du_ref, dr_ref
+):
     tile = x0_ref.shape[-1]
     x0 = x0_ref[...].reshape(-1, tile).T
     x1 = x1_ref[...].reshape(-1, tile).T
     dg_ref[0] = dot(x0, g0_ref[0]) + dot(x1, g1_ref[0])
     du_ref[0] = dot(x0, u0_ref[0]) + dot(x1, u1_ref[0])
-
-
-def wide_grad(xs, gslopes, uslopes, halves):
+    dr_ref[0] = dot(x0, l0_ref[0]) + dot(x1, l1_ref[0])
+
+
+def wide_grad(xs, gslopes, uslopes, logit_slopes, halves):
     planes, local, slots, width = xs[0].shape
     units, count, hidden = gslopes[0].shape
     tile = 1024 if planes * slots <= 1024 else 512
@@ -1347,16 +1365,21 @@
     s_spec = pl.BlockSpec((1, count, hidden), lambda u, j: (u, 0, 0))
     o_spec = pl.BlockSpec((1, tile, hidden), lambda u, j: (u, j, 0))
     out = shape_of((units, width, hidden), F32)
+    experts_all = logit_slopes[0].shape[2]
     return pl.pallas_call(
         wide_grad_kernel,
         grid=(units, width // tile),
-        out_shape=(out, out),
-        in_specs=[x_spec] * 2 + [s_spec] * 4,
-        out_specs=(o_spec, o_spec),
+        out_shape=(out, out, shape_of((local, width, experts_all), F32)),
+        in_specs=[x_spec] * 2
+        + [s_spec] * 4
+        + [pl.BlockSpec((1, count, experts_all), lambda u, j: (u // halves, 0, 0))] * 2,
+        out_specs=(
+            o_spec, o_spec, pl.BlockSpec((1, tile, experts_all), lambda u, j: (u // halves, j, 0)),
+        ),
         compiler_params=params(60),
         cost_estimate=cost(8 * units * count * hidden * width, 8 * units * hidden * width),
         name="wide_grad",
-    )(*xs, *gslopes, *uslopes)
+    )(*xs, *gslopes, *uslopes, *logit_slopes)
 
 
 def down_grad_kernel(a0_ref, a1_ref, ca_ref, cb_ref, d_ref):
@@ -1496,18 +1519,18 @@
     attention_parts = [chunk(attention_part, k) for k in range(CHUNKS)]
     arrived_slopes = [swap_plane(rows)]
     rows = dispatch(by_pair, incoming[1], planes, local, slots)
-    attended, swapped = line_swap(attention_parts[0], rows, line, 4)
+    held, normed, swapped = hide(
+        attention_parts[0], block_in, gain_second[None], rows, 0, line, 4
+    )
     arrived_slopes.append(swapped)
-    hidden, arrived = block_in, []
-    for k in range(CHUNKS):
-        hidden, normed = hide(block_in, attended, gain_second[None], k * chunk_rows, tokens, hidden)
-        rows = dispatch(by_pair[k:k + 1], normed, planes, local, slots)
-        if k + 1 < CHUNKS:
-            attended, swapped = line_swap(attention_parts[k + 1], rows, line, 3)
-            arrived.append(swapped)
-        else:
-            rows, arrived_slopes[0] = lax.optimization_barrier((rows, arrived_slopes[0]))
-            arrived.append(swap_plane(rows))
+    rows = dispatch(by_pair[:1], normed, planes, local, slots)
+    held_next, normed, swapped = hide(
+        attention_parts[1], block_in, gain_second[None], rows, 1, line, 3
+    )
+    hidden, arrived = [held, held_next], [swapped]
+    rows = dispatch(by_pair[1:], normed, planes, local, slots)
+    rows, arrived_slopes[0] = lax.optimization_barrier((rows, arrived_slopes[0]))
+    arrived.append(swap_plane(rows))
     weighted = arrived_slopes[0]
     row_slopes, acts, gslopes, uslopes, logit_slopes = [], [], [], [], []
     for k in range(CHUNKS):
@@ -1525,20 +1548,22 @@
         behind = swap_plane(rows)
         returned.append(behind)
 
-    second_gain_grad = 0.0
-    kept = (block_in,) * 3
+    hidden_slopes, attention_slopes, blended_slopes, second_parts = [], [], [], []
     for k in range(CHUNKS):
-        returned[k], _ = lax.optimization_barrier((returned[k], summed if k else row_slopes[-1]))
+        returned[k], _ = lax.optimization_barrier(
+            (returned[k], hidden_slopes[0] if k else row_slopes[-1])
+        )
         part = combine(by_token[k:k + 1], returned[k], slots)
         if k:
             rows, _ = lax.optimization_barrier((weighted, returned[k]))
             mixed_rows = swap_plane(rows)
-        summed = line_sum(part, line)
-        *kept, gain_part = hide_back(
-            summed, hidden, incoming, gain_second[None], output_weight, k * chunk_rows, tokens, kept
-        )
-        second_gain_grad = second_gain_grad + gain_part
-    hidden_slope, attention_slope, blended_slope = kept
+        results = hide_back(part, hidden[k], incoming, gain_second[None], k, line)
+        for store, result in zip((hidden_slopes, attention_slopes, second_parts), results):
+            store.append(result)
+    second_gain_grad = second_parts[0] + second_parts[1]
+    blended_slope = jnp.concatenate(
+        [contract("td,cd->tc", low, output_weight).astype(BF) for low in attention_slopes]
+    )
     slopes = attend_back(
         query_low, key_low, value_low, blended_slope, log_total, start_row,
         place_row, place_column, own_heads, tokens,
@@ -1547,22 +1572,16 @@
     dots = small_line_sum(dots, line)
     mixed_rows, _ = lax.optimization_barrier((mixed_rows, gain_grads))
     mixed = combine(by_token, mixed_rows, slots)
-    acts, gslopes, uslopes, logit_slopes, attention_slope, _ = lax.optimization_barrier(
-        (acts, gslopes, uslopes, logit_slopes, attention_slope, mixed)
+    acts, gslopes, uslopes, logit_slopes, attention_slopes, _ = lax.optimization_barrier(
+        (acts, gslopes, uslopes, logit_slopes, attention_slopes, mixed)
     )
     mixed = lax.psum_scatter(mixed, "fsdp", scatter_dimension=0, tiled=True)
-    expert_grads = [
-        *wide_grad(arrived, gslopes, uslopes, halves),
-        down_grad(acts, arrived_slopes, halves),
-    ]
-    router_grad = sum(
-        contract(
-            "ensd,nesq->dq", arrived[k],
-            logit_slopes[k].reshape(local, planes, slots, expert_count),
-        )
-        for k in range(CHUNKS)
-    )
-    output_grad = contract("tc,td->cd", blended, attention_slope).astype(BF)
+    *expert_grads, router_parts = wide_grad(arrived, gslopes, uslopes, logit_slopes, halves)
+    expert_grads.append(down_grad(acts, arrived_slopes, halves))
+    router_grad = jnp.sum(router_parts, axis=0)
+    output_grad = sum(
+        contract("tc,td->cd", chunk(blended, k), attention_slopes[k]) for k in range(CHUNKS)
+    ).astype(BF)
     dots, _ = lax.optimization_barrier((dots, expert_grads))
     joint, normed_part = join_slopes(
         *slopes, raw, squares, dots, both_gains, *rotary, columns, tokens
@@ -1581,9 +1600,12 @@
     input_gradient, totals, output_total, gain_totals = finish(
         normed_part, joint_total.reshape(line, planes, slice_rows, -1),
         output_grad.reshape(planes, slice_rows, width), inputs, gain_first[None],
-        hidden_slope, gain_rows, planes, line,
-    )
-    hidden_own = lax.dynamic_slice_in_dim(hidden, line_at * tokens, tokens, 0)
+        hidden_slopes, gain_rows, planes, line,
+    )
+    start = (line_at % blocks) * tokens
+    hidden_own = jnp.where(
+        line_at < blocks, *(lax.dynamic_slice_in_dim(held, start, tokens, 0) for held in hidden)
+    )
     block_output = (hidden_own + mixed.astype(F32)).astype(BF)
     *weight_grads, router_total = widen(
         totals.reshape(line, planes // 2, 2, slice_rows, -1),

time: 1280 us -> 1260 us (0.984)
  Pallas kernels: 1120 us -> 1100 us
    pallas_call x8 -> x4, Pallas kernels: 375 us -> 341 us  [the longest x2 172 us: hide(): pl.pallas_call(functools.partial(hide_kernel, planes, line, pieces, lag,...]
  transfers between devices with their start and end apart: 13 -> 13, of which waited for: 6 -> 3; matrix products, arithmetic and copies ran while one was open for 3% -> 3% of each run, Pallas kernels for 71% -> 71%
where the time goes in v1:
time: 1260 us; the launch traced here: 1250 us
  Pallas kernels  1100 us (87%)
  local copies, waits for them, and re-layouts  47.1 us (4%)
  starting transfers between devices  33.2 us (3%)
  matrix products  21.2 us (2%)
  waiting for transfers between devices  18.2 us (1%)
  other arithmetic  17.5 us (1%)
  between operations  15.2 us (1%)
    pallas_call x1, Pallas kernels, gather_start(): pl.pallas_call(functools.partial(gather_kernel, planes, line, pieces), ou...  190 us
    pallas_call x2, Pallas kernels, hide(): pl.pallas_call(functools.partial(hide_kernel, planes, line, pieces, lag,...  172 us
    pallas_call x2, Pallas kernels, hide_back(): pl.pallas_call(functools.partial(hide_back_kernel, line, pieces, lag, at)...  170 us
    pallas_call x2, Pallas kernels, experts(): pl.pallas_call(functools.partial(expert_kernel, halves), grid=(local, ste...  161 us
    pallas_call x1, Pallas kernels, finish(): pl.pallas_call(functools.partial(finish_kernel, planes, line, height, lag...  139 us
    pallas_call x1, Pallas kernels, wide_grad(): pl.pallas_call(wide_grad_kernel, grid=(units, width // tile), out_shape=(...  49.1 us
    pallas_call x1, Pallas kernels, attend_back(): pl.pallas_call(functools.partial(attend_back_kernel, size), grid=(heads /...  37.6 us
    pallas_call x3, Pallas kernels, combine(): pl.pallas_call(functools.partial(combine_kernel, slots), grid=(chunks, wi...  37.5 us
  transfers between devices with their start and end apart: 13, of which 3 were waited for; matrix products, arithmetic and copies ran while one was open for 3% of the time, Pallas kernels for 71%

profile of v1, /device:TPU:0, one launch (start us, length us, event | category | flops | bytes accessed | tf_op | source)
XLA Modules:
  0.0 1253.9 jit_solution(599429495894417885)
XLA Ops:
  14.3 189.9 %gather_start.1 = (bf16[1536,2048]{1,0:T(8,128)(2,1)}, bf16[1536,1024]{1,0:T(8,128)(2,1)}, bf16[1152,128]{1,0:T(8,128)(2,1)}, bf16[4,8,64,1536]{3,2,1,0:T(8,128)(2,1)}, bf16[4,64,1536]{2,1,0:T(8,128)(2,1)}) custom-call(bf16[384,2048]{1,0:T(8,128)(2,1)} %x_ref.3, bf16[384,2048]{1,0:T(8,128)(2,1)} %c_ref.1, bf16[288,128]{1,0:T(8,128)(2,1)} %maximum_bitcast_fusion.1.small_ref, ...), custom_call_target="tpu_custom_call" | custom-call | tf_op jit(solution)/shard_map/gather_start/pallas_call | solution.py:192
  212.6 8.9 dispatch.7
  221.4 5.0 all-to-all-start
  227.5 15.5 %project.1 = (bf16[1536,2048]{1,0:T(8,128)(2,1)}, f32[1536,1024]{1,0:T(8,128)}, bf16[1536,512]{1,0:T(8,128)(2,1)S(1)}, f32[2,1536]{1,0:T(2,128)S(1)}) custom-call(bf16[1536,2048]{1,0:T(8,128)(2,1)} %get-tuple-element.89.x_ref, f32[1,2048]{1,0:T(1,128)S(1)} %bitcast.56, bf16[2048,1536]{1,0:T(8,128)(2,1)} %bitcast.59), custom_call_target="tpu_custom_call" | custom-call | flops 150994944 | bytes 172032 | tf_op jit(solution)/shard_map/project/pallas_call | solution.py:895
  244.2 3.0 collective-permute-start.1
  248.6 2.8 fusion.10
  255.0 2.5 turn.1
  259.8 21.7 %attend.1 = (bf16[1536,512]{1,0:T(8,128)(2,1)}, f32[4,1,1536]{2,1,0:T(1,128)}) custom-call(bf16[1536,512]{1,0:T(8,128)(2,1)} %copy-done.6, bf16[1536,512]{1,0:T(8,128)(2,1)} %copy-done.7, bf16[1536,512]{1,0:T(8,128)(2,1)} %copy-done.5, s32[1,1536]{1,0:T(1,128)} %broadcast_in_dim.20.start_ref, s32[1,1536]{1,0:T(1,128)} %broadcast_in_dim.21.place_ref, ...), custom_call_target="tpu_custom_call" | custom-call | flops 301989888 | bytes 98304 | tf_op jit(solution)/shard_map/attend/pallas_call | solution.py:1059
  281.5 5.1 convolution_convert_fusion
  286.5 3.3 fusion.19
  289.8 4.6 all-gather.2.cloned.1.call-done.rows_ref.cb_ref
  294.4 1.9 copy-done.3
  296.3 8.8 dispatch.4.rows_ref
  305.1 86.1 %hide.2 = (f32[768,2048]{1,0:T(8,128)}, bf16[768,2048]{1,0:T(8,128)(2,1)}, bf16[8,2,224,1024]{3,2,1,0:T(8,128)(2,1)}) custom-call(bf16[768,2048]{1,0:T(8,128)(2,1)} %get-tuple-element.206.p_ref, bf16[1536,2048]{1,0:T(8,128)(2,1)} %get-tuple-element.89.x_ref, f32[1,2048]{1,0:T(1,128)} %bitcast.62, bf16[8,2,224,1024]{3,2,1,0:T(8,128)(2,1)} %dispatch.4.rows_ref), custom_call_target="tpu_custom_call" | custom-call | bytes 4915200 | tf_op jit(solution)/shard_map/hide/pallas_call | solution.py:394
  391.2 1.9 copy-done.13
  393.1 8.4 dispatch.5.rows_ref
  401.5 85.9 %hide.3 = (f32[768,2048]{1,0:T(8,128)}, bf16[768,2048]{1,0:T(8,128)(2,1)}, bf16[8,2,112,2048]{3,2,1,0:T(8,128)(2,1)}) custom-call(bf16[768,2048]{1,0:T(8,128)(2,1)} %get-tuple-element.207.p_ref, bf16[1536,2048]{1,0:T(8,128)(2,1)} %get-tuple-element.89.x_ref, f32[1,2048]{1,0:T(1,128)} %bitcast.63, bf16[8,2,112,2048]{3,2,1,0:T(8,128)(2,1)} %dispatch.5.rows_ref), custom_call_target="tpu_custom_call" | custom-call | bytes 4915200 | tf_op jit(solution)/shard_map/hide/pallas_call | solution.py:394
  487.4 1.9 copy-done.12
  489.2 8.4 dispatch.6
  497.6 4.9 all-to-all-start.1
  504.5 84.6 %experts.2 = (bf16[8,2,224,2048]{3,2,1,0:T(8,128)(2,1)}, bf16[8,2,112,2048]{3,2,1,0:T(8,128)(2,1)}, bf16[4,896,512]{2,1,0:T(8,128)(2,1)}, bf16[4,896,512]{2,1,0:...) custom-call(bf16[8,2,112,2048]{3,2,1,0:T(8,128)(2,1)} %get-tuple-element.107.x_ref.x0_ref, ...), custom_call_target="tpu_custom_call" | custom-call | flops 704643072 | bytes 573440 | tf_op jit(solution)/shard_map/experts/pallas_call | solution.py:1324
  589.1 4.9 all-to-all-start.2
  594.0 76.3 %experts.3 = (bf16[8,2,224,2048]{3,2,1,0:T(8,128)(2,1)}, bf16[8,2,112,2048]{3,2,1,0:T(8,128)(2,1)}, bf16[4,896,512]{2,1,0:T(8,128)(2,1)}, bf16[4,896,512]{2,1,0:...) custom-call(bf16[8,2,112,2048]{3,2,1,0:T(8,128)(2,1)} %all-to-all-done.1, ...), custom_call_target="tpu_custom_call", output_to_operand_aliasing={{0}: (8, {})} | custom-call | flops 704643072 | bytes 573440 | tf_op jit(solution)/shard_map/experts/pallas_call | solution.py:1324
  670.4 6.5 all-to-all-done.2.rows_ref
  676.8 5.0 all-to-all-start.3
  682.9 9.8 combine.3.p_ref
  692.8 84.7 %hide_back.2 = (f32[768,2048]{1,0:T(8,128)}, bf16[768,2048]{1,0:T(8,128)(2,1)}, f32[1,2048]{1,0:T(1,128)}) custom-call(bf16[768,2048]{1,0:T(8,128)(2,1)} %combine.3.p_ref, f32[768,2048]{1,0:T(8,128)} %get-tuple-element.99.hidden_ref, bf16[1536,1024]{1,0:T(8,128)(2,1)} %get-tuple-element.103.rows_ref.ca_ref, ...), custom_call_target="tpu_custom_call" | custom-call | bytes 4259840 | tf_op jit(solution)/shard_map/hide_back/pallas_call | solution.py:465
  777.5 5.6 all-to-all-start.4
  783.1 5.2 convolution_convert_fusion.2
  788.4 9.8 combine.4.p_ref
  798.2 84.8 %hide_back.3 = (f32[768,2048]{1,0:T(8,128)}, bf16[768,2048]{1,0:T(8,128)(2,1)}, f32[1,2048]{1,0:T(1,128)}) custom-call(bf16[768,2048]{1,0:T(8,128)(2,1)} %combine.4.p_ref, f32[768,2048]{1,0:T(8,128)} %get-tuple-element.101.hidden_ref, bf16[1536,1024]{1,0:T(8,128)(2,1)} %get-tuple-element.103.rows_ref.ca_ref, ...), custom_call_target="tpu_custom_call" | custom-call | bytes 4259840 | tf_op jit(solution)/shard_map/hide_back/pallas_call | solution.py:465
  883.0 4.4 convolution_convert_fusion.1
  888.7 37.6 %attend_back.1 = (bf16[1536,512]{1,0:T(8,128)(2,1)}, bf16[1536,512]{1,0:T(8,128)(2,1)}, bf16[1536,512]{1,0:T(8,128)(2,1)}) custom-call(bf16[1536,512]{1,0:T(8,128)(2,1)} %copy-done.6, bf16[1536,512]{1,0:T(8,128)(2,1)} %copy-done.7, bf16[1536,512]{1,0:T(8,128)(2,1)} %copy-done.5, bf16[1536,512]{1,0:T(8,128)(2,1)} %pad_maximum_fusion.g_ref, ...), custom_call_target="tpu_custom_call" | custom-call | flops 566231040 | bytes 196608 | tf_op jit(solution)/shard_map/attend_back/pallas_call | solution.py:1117
  926.3 2.8 copy-done.1
  931.9 5.6 turn_back.1
  937.5 7.1 all-to-all-done.4.rows_ref
  944.6 17.8 %combine.5 = bf16[1536,2048]{1,0:T(8,128)(2,1)} custom-call(bf16[2,768,16]{2,1,0:T(8,128)(2,1)} %copy-done.17, bf16[8,2,224,2048]{3,2,1,0:T(8,128)(2,1)} %all-to-all-done.4.rows_ref), custom_call_target="tpu_custom_call" | custom-call | flops 176160768 | bytes 229376 | tf_op jit(solution)/shard_map/combine/pallas_call | solution.py:1250
  963.4 3.0 collective-permute-start.5
  969.0 27.4 %down_grad.1 = f32[4,512,2048]{2,1,0:T(8,128)} custom-call(bf16[4,896,512]{2,1,0:T(8,128)(2,1)} %get-tuple-element.143.a0_ref, bf16[4,896,512]{2,1,0:T(8,128)(2,1)} %get-tuple-element.144.a1_ref, bf16[8,2,224,1024]{3,2,1,0:T(8,128)(2,1)} %all-to-all-done.ca_ref.kept_ref, bf16[8,2,224,1024]{3,2,1,0:T(8,128)(2,1)} %get-tuple-element.106.cb_ref), custom_call_target="tpu_custom_call" | custom-call | flops 234881024 | bytes 262144 | tf_op jit(solution)/shard_map/down_grad/pallas_call | solution.py:1405
  996.4 49.1 %wide_grad.1 = (f32[4,2048,512]{2,1,0:T(8,128)}, f32[4,2048,512]{2,1,0:T(8,128)}, f32[2,2048,64]{2,1,0:T(8,128)}) custom-call(bf16[8,2,112,2048]{3,2,1,0:T(8,128)(2,1)} %get-tuple-element.107.x_ref.x0_ref, bf16[8,2,112,2048]{3,2,1,0:T(8,128)(2,1)} %all-to-all-done.1.x_ref.x1_ref, bf16[4,896,512]{2,1,0:T(8,128)(2,1)} %get-tuple-element.135.g0_ref, ...), custom_call_target="tpu_custom_call" | custom-call | flops 469762048 | bytes 524288 | tf_op jit(solution)/shard_map/wide_grad/pallas_call | solution.py:1369
  1045.5 2.1 reduce_sum.29
  1051.3 17.2 %join_slopes.1 = (bf16[1536,1536]{1,0:T(8,128)(2,1)}, bf16[1536,2048]{1,0:T(8,128)(2,1)}) custom-call(bf16[1536,512]{1,0:T(8,128)(2,1)S(1)} %copy-done.9, bf16[1536,512]{1,0:T(8,128)(2,1)S(1)} %copy-done.11, bf16[1536,512]{1,0:T(8,128)(2,1)} %get-tuple-element.125.dv_ref, f32[1536,1024]{1,0:T(8,128)} %get-tuple-element.92.raw_ref, ...), custom_call_target="tpu_custom_call" | custom-call | flops 150994944 | bytes 393216 | tf_op jit(solution)/shard_map/join_slopes/pallas_call | solution.py:1017
  1068.5 15.2 %joint_grad.1 = bf16[2048,1664]{1,0:T(8,128)(2,1)} custom-call(bf16[1536,2048]{1,0:T(8,128)(2,1)} %get-tuple-element.147.normed_ref, bf16[1536,1536]{1,0:T(8,128)(2,1)} %get-tuple-element.148.joint_ref, bf16[2048,128]{1,0:T(8,128)(2,1)} %pad.4.router_ref), custom_call_target="tpu_custom_call" | custom-call | flops 150994944 | bytes 294912 | tf_op jit(solution)/shard_map/joint_grad/pallas_call | solution.py:1179
  1085.6 3.2 add_convert_fusion
  1088.7 138.9 %finish.1 = (bf16[384,2048]{1,0:T(8,128)(2,1)}, bf16[4,8,64,1664]{3,2,1,0:T(8,128)(2,1)}, bf16[8,64,2048]{2,1,0:T(8,128)(2,1)}, f32[8,512]{1,0:T(8,128)}) custom-call(bf16[1536,2048]{1,0:T(8,128)(2,1)} %get-tuple-element.146.p_ref, bf16[4,4,2,64,1664]{4,3,2,1,0:T(8,128)(2,1)} %bitcast.58, bf16[4,2,64,2048]{3,2,1,0:T(8,128)(2,1)} %bitcast.61, ...), custom_call_target="tpu_custom_call" | custom-call | bytes 6553600 | tf_op jit(solution)/shard_map/finish/pallas_call | solution.py:823
  1227.7 2.9 copy-done.4
  1232.2 6.4 widen.1
  1240.0 5.4 add_convert_fusion.1
  (145 shorter events, 45.0 us)
Async XLA Ops:
  8.7 4.4 copy-start.24
  9.7 3.7 copy-start.25
  9.7 4.0 copy-start.27
  9.7 4.0 copy-start.28
  204.2 8.4 copy-start.2
  221.4 5.0 copy-start.16
  221.4 276.2 %all-to-all-start = ((bf16[8,2,224,1024]{3,2,1,0:T(8,128)(2,1)}), bf16[8,2,224,1024]{3,2,1,0:T(8,128)(2,1)}, u32[]{:S(2)}, u32[]{:S(2)}) async-start(bf16[8,2,224,1024]{3,2,1,0:T(8,128)(2,1)} %dispatch.7), calls=%async_computation | async-start | bytes 14680064 | tf_op jit(solution)/shard_map/all_to_all | solution.py:856
  226.4 68.0 %all-gather.2.cloned.1.call-start = ((), (), s32[]{:S(2)}) async-start(), calls=%async_computation.6 | async-start | bytes 3932160 | tf_op jit(solution)/shard_map/all_gather | solution.py:1481
  227.5 15.6 %copy-start.15 = (f32[1,1,4,512]{3,1,2,0:T(1,128)}, f32[1,1,4,512]{3,1,2,0:T(1,128)S(1)}, u32[]{:S(2)}) copy-start(f32[1,1,4,512]{3,1,2,0:T(1,128)S(1)} %copy.58) | copy-start | bytes 24580
  227.5 20.8 %copy-start.31 = (s32[1,2]{1,0:T(1,128)S(1)}, s32[1,2]{1,0:T(1,128)}, u32[]{:S(2)}) copy-start(s32[1,2]{1,0:T(1,128)} %param.31) | copy-start | bytes 28
  227.5 21.0 %copy-start.29 = (bf16[512]{0:T(512)(128)(2,1)S(1)}, bf16[512]{0:T(512)(128)(2,1)}, u32[]{:S(2)}) copy-start(bf16[512]{0:T(512)(128)(2,1)} %param.24) | copy-start | bytes 3076
  227.5 20.9 %copy-start.30 = (bf16[512]{0:T(512)(128)(2,1)S(1)}, bf16[512]{0:T(512)(128)(2,1)}, u32[]{:S(2)}) copy-start(bf16[512]{0:T(512)(128)(2,1)} %param.25) | copy-start | bytes 3076
  227.5 21.0 %copy-start.23 = (s32[1536]{0:T(1024)S(1)}, s32[1536]{0:T(1024)}, u32[]{:S(2)}) copy-start(s32[1536]{0:T(1024)} %param.32) | copy-start | bytes 18436
  243.1 1.2 copy-start.5
  244.2 10.7 collective-permute-start
  244.2 10.7 collective-permute-start.1
  247.3 7.7 collective-permute-start.2
  248.6 6.3 copy-start
  257.5 1.1 copy-start.6
  258.6 1.1 copy-start.7
  259.8 21.7 %copy-start.33 = (bf16[512,2048]{1,0:T(8,128)(2,1)S(1)}, bf16[512,2048]{1,0:T(8,128)(2,1)}, u32[]{:S(2)}) copy-start(bf16[512,2048]{1,0:T(8,128)(2,1)} %param.21) | copy-start | bytes 6291460
  294.4 1.9 copy-start.3
  391.2 1.9 copy-start.13
  487.3 1.9 copy-start.12
  497.6 91.5 %all-to-all-start.1 = ((bf16[8,2,112,2048]{3,2,1,0:T(8,128)(2,1)}), bf16[8,2,112,2048]{3,2,1,0:T(8,128)(2,1)}, u32[]{:S(2)}, u32[]{:S(2)}) async-start(bf16[8,2,112,2048]{3,2,1,0:T(8,128)(2,1)} %dispatch.6), calls=%async_computation.1 | async-start | bytes 14680064 | tf_op jit(solution)/shard_map/all_to_all | solution.py:856
  589.1 87.7 %all-to-all-start.2 = ((bf16[8,2,112,2048]{3,2,1,0:T(8,128)(2,1)}), bf16[8,2,112,2048]{3,2,1,0:T(8,128)(2,1)}, u32[]{:S(2)}, u32[]{:S(2)}) async-start(bf16[8,2,112,2048]{3,2,1,0:T(8,128)(2,1)} %get-tuple-element.112), calls=%async_computation.2 | async-start | bytes 14680064 | tf_op jit(solution)/shard_map/all_to_all | solution.py:856
  676.8 5.0 copy-start.20
  676.8 100.7 %all-to-all-start.3 = ((bf16[8,2,112,2048]{3,2,1,0:T(8,128)(2,1)}), bf16[8,2,112,2048]{3,2,1,0:T(8,128)(2,1)}, u32[]{:S(2)}, u32[]{:S(2)}) async-start(bf16[8,2,112,2048]{3,2,1,0:T(8,128)(2,1)} %get-tuple-element.113), calls=%async_computation.3 | async-start | bytes 14680064 | tf_op jit(solution)/shard_map/all_to_all | solution.py:856
  682.1 10.7 copy-start.17
  777.5 167.1 %all-to-all-start.4 = ((bf16[8,2,224,2048]{3,2,1,0:T(8,128)(2,1)}), bf16[8,2,224,2048]{3,2,1,0:T(8,128)(2,1)}, u32[]{:S(2)}, u32[]{:S(2)}) async-start(bf16[8,2,224,2048]{3,2,1,0:T(8,128)(2,1)} %get-tuple-element.117), calls=%async_computation.4 | async-start | bytes 29360128 | tf_op jit(solution)/shard_map/all_to_all | solution.py:856
  783.1 456.9 %reduce-scatter.2.cloned.1.call-start = ((), (), s32[]{:S(2)}) async-start(), calls=%async_computation.7 | async-start | bytes 7864320 | tf_op jit(solution)/shard_map/reduce_scatter | solution.py:1578
  883.0 4.4 copy-start.21
  926.3 2.8 copy-start.1
  929.1 1.4 copy-start.8
  930.5 1.4 copy-start.10
  962.5 6.4 collective-permute-start.3
  962.6 6.4 collective-permute-start.4
  963.4 5.6 collective-permute-start.5
  1048.4 1.4 copy-start.9
  1049.8 1.4 copy-start.11
  1068.5 15.2 %copy-start.18 = (bf16[768,2048]{1,0:T(8,128)(2,1)S(1)}, bf16[768,2048]{1,0:T(8,128)(2,1)}, u32[]{:S(2)}) copy-start(bf16[768,2048]{1,0:T(8,128)(2,1)} %get-tuple-element.150) | copy-start | bytes 9437188
  1068.5 15.2 %copy-start.22 = (bf16[1536,512]{1,0:T(8,128)(2,1)S(1)}, bf16[1536,512]{1,0:T(8,128)(2,1)}, u32[]{:S(2)}) copy-start(bf16[1536,512]{1,0:T(8,128)(2,1)} %get-tuple-element.97) | copy-start | bytes 4718596
  1083.7 1.9 copy-start.32
  1227.7 2.9 copy-start.4
  1230.6 1.6 copy-start.14
  1232.2 7.2 copy-start.26
  1240.0 5.4 copy-start.19
Sparse Core Ops, SparseCore 0:
  229.4 64.9 all-gather.1
  962.6 107.4 reduce-scatter.1

commit v2 on v1

--- a/solution.py
+++ b/solution.py
@@ -1192,18 +1192,24 @@
     )(normed, joint, router)
 
 
-def dispatch_kernel(slots, code_ref, rows_ref, o_ref, select):
+def dispatch_kernel(code_ref, rows_ref, o_ref, select):
     pairs = code_ref.shape[1]
+    blocks, _, tokens = select.shape
+    tile = rows_ref.shape[1]
 
     @pl.when(pl.program_id(1) == 0)
     def _():
-        for i in range(pairs):
-            row = code_ref[0, i:i + 1, :]
-            slot = lax.broadcasted_iota(jnp.int32, (slots, row.shape[1]), 0).astype(F32)
-            select[i * slots:(i + 1) * slots, :] = (slot == row).astype(BF)
-
-    chosen = dot(select[...], rows_ref[...]).astype(BF)
-    o_ref[...] = chosen.reshape(o_ref.shape)
+        for b in range(blocks):
+            row = code_ref[0, :, b * tokens:(b + 1) * tokens][:, None, :]
+            slot = lax.broadcasted_iota(jnp.int32, (pairs, CAP, tokens), 1) + b * CAP
+            chosen = jnp.where(slot.astype(F32) == row, 1.0, 0.0)
+            select[b] = chosen.reshape(pairs * CAP, tokens).astype(BF)
+
+    parts = [
+        dot(select[b], rows_ref[b * tokens:(b + 1) * tokens, :]).reshape(pairs, CAP, tile)
+        for b in range(blocks)
+    ]
+    o_ref[...] = jnp.concatenate(parts, axis=1).astype(BF).reshape(o_ref.shape)
 
 
 def dispatch(codes, rows, planes, local, slots):
@@ -1211,7 +1217,7 @@
     width = rows.shape[1]
     tile = 512
     return pl.pallas_call(
-        functools.partial(dispatch_kernel, slots),
+        dispatch_kernel,
         grid=(chunks, width // tile),
         out_shape=shape_of((planes, local, chunks * slots, width), BF),
         in_specs=[
@@ -1219,7 +1225,7 @@
             pl.BlockSpec((count, tile), lambda k, j: (k, j)),
         ],
         out_specs=pl.BlockSpec((planes, local, slots, tile), lambda k, j: (0, 0, k, j)),
-        scratch_shapes=[pltpu.VMEM((pairs * slots, count), BF)],
+        scratch_shapes=[pltpu.VMEM((slots // CAP, pairs * CAP, count * CAP // slots), BF)],
         compiler_params=params(48),
         cost_estimate=cost(2 * pairs * slots * chunks * count * width, 4 * pairs * slots * width),
         name="dispatch",
@@ -1352,8 +1358,9 @@
     tile = x0_ref.shape[-1]
     x0 = x0_ref[...].reshape(-1, tile).T
     x1 = x1_ref[...].reshape(-1, tile).T
-    dg_ref[0] = dot(x0, g0_ref[0]) + dot(x1, g1_ref[0])
-    du_ref[0] = dot(x0, u0_ref[0]) + dot(x1, u1_ref[0])
+    for h in range(dg_ref.shape[0]):
+        dg_ref[h] = dot(x0, g0_ref[h]) + dot(x1, g1_ref[h])
+        du_ref[h] = dot(x0, u0_ref[h]) + dot(x1, u1_ref[h])
     dr_ref[0] = dot(x0, l0_ref[0]) + dot(x1, l1_ref[0])
 
 
@@ -1361,20 +1368,20 @@
     planes, local, slots, width = xs[0].shape
     units, count, hidden = gslopes[0].shape
     tile = 1024 if planes * slots <= 1024 else 512
-    x_spec = pl.BlockSpec((planes, 1, slots, tile), lambda u, j: (0, u // halves, 0, j))
-    s_spec = pl.BlockSpec((1, count, hidden), lambda u, j: (u, 0, 0))
-    o_spec = pl.BlockSpec((1, tile, hidden), lambda u, j: (u, j, 0))
+    x_spec = pl.BlockSpec((planes, 1, slots, tile), lambda n, j: (0, n, 0, j))
+    s_spec = pl.BlockSpec((halves, count, hidden), lambda n, j: (n, 0, 0))
+    o_spec = pl.BlockSpec((halves, tile, hidden), lambda n, j: (n, j, 0))
     out = shape_of((units, width, hidden), F32)
     experts_all = logit_slopes[0].shape[2]
     return pl.pallas_call(
         wide_grad_kernel,
-        grid=(units, width // tile),
+        grid=(local, width // tile),
         out_shape=(out, out, shape_of((local, width, experts_all), F32)),
         in_specs=[x_spec] * 2
         + [s_spec] * 4
-        + [pl.BlockSpec((1, count, experts_all), lambda u, j: (u // halves, 0, 0))] * 2,
+        + [pl.BlockSpec((1, count, experts_all), lambda n, j: (n, 0, 0))] * 2,
         out_specs=(
-            o_spec, o_spec, pl.BlockSpec((1, tile, experts_all), lambda u, j: (u // halves, j, 0)),
+            o_spec, o_spec, pl.BlockSpec((1, tile, experts_all), lambda n, j: (n, j, 0)),
         ),
         compiler_params=params(60),
         cost_estimate=cost(8 * units * count * hidden * width, 8 * units * hidden * width),

time: 1260 us -> 1250 us (level)
  Pallas kernels: 1100 us -> 1080 us
  transfers between devices with their start and end apart: 13 -> 13, of which waited for: 3 -> 4; matrix products, arithmetic and copies ran while one was open for 3% -> 3% of each run, Pallas kernels for 71% -> 70%
where the time goes in v2:
time: 1250 us; the launch traced here: 1240 us
  Pallas kernels  1080 us (86%)
  local copies, waits for them, and re-layouts  47.1 us (4%)
  starting transfers between devices  33.4 us (3%)
  waiting for transfers between devices  22.9 us (2%)
  matrix products  21.2 us (2%)
  other arithmetic  17.6 us (1%)
  between operations  14.9 us (1%)
    pallas_call x1, Pallas kernels, gather_start(): pl.pallas_call(functools.partial(gather_kernel, planes, line, pieces), ou...  190 us
    pallas_call x2, Pallas kernels, hide(): pl.pallas_call(functools.partial(hide_kernel, planes, line, pieces, lag,...  172 us
    pallas_call x2, Pallas kernels, hide_back(): pl.pallas_call(functools.partial(hide_back_kernel, line, pieces, lag, at)...  169 us
    pallas_call x2, Pallas kernels, experts(): pl.pallas_call(functools.partial(expert_kernel, halves), grid=(local, ste...  152 us
    pallas_call x1, Pallas kernels, finish(): pl.pallas_call(functools.partial(finish_kernel, planes, line, height, lag...  139 us
    pallas_call x1, Pallas kernels, wide_grad(): pl.pallas_call(wide_grad_kernel, grid=(local, width // tile), out_shape=(...  47.2 us
    pallas_call x1, Pallas kernels, attend_back(): pl.pallas_call(functools.partial(attend_back_kernel, size), grid=(heads /...  37.6 us
    pallas_call x3, Pallas kernels, combine(): pl.pallas_call(functools.partial(combine_kernel, slots), grid=(chunks, wi...  37.5 us
  transfers between devices with their start and end apart: 13, of which 4 were waited for; matrix products, arithmetic and copies ran while one was open for 3% of the time, Pallas kernels for 70%

profile of v2, /device:TPU:0, one launch (start us, length us, event | category | flops | bytes accessed | tf_op | source)
XLA Modules:
  0.0 1239.0 jit_solution(13458838416969583155)
XLA Ops:
  14.3 189.9 %gather_start.1 = (bf16[1536,2048]{1,0:T(8,128)(2,1)}, bf16[1536,1024]{1,0:T(8,128)(2,1)}, bf16[1152,128]{1,0:T(8,128)(2,1)}, bf16[4,8,64,1536]{3,2,1,0:T(8,128)(2,1)}, bf16[4,64,1536]{2,1,0:T(8,128)(2,1)}) custom-call(bf16[384,2048]{1,0:T(8,128)(2,1)} %x_ref.3, bf16[384,2048]{1,0:T(8,128)(2,1)} %c_ref.1, bf16[288,128]{1,0:T(8,128)(2,1)} %maximum_bitcast_fusion.1.small_ref, ...), custom_call_target="tpu_custom_call" | custom-call | tf_op jit(solution)/shard_map/gather_start/pallas_call | solution.py:192
  212.6 6.6 dispatch.7
  219.1 5.0 all-to-all-start
  225.2 15.5 %project.1 = (bf16[1536,2048]{1,0:T(8,128)(2,1)}, f32[1536,1024]{1,0:T(8,128)}, bf16[1536,512]{1,0:T(8,128)(2,1)S(1)}, f32[2,1536]{1,0:T(2,128)S(1)}) custom-call(bf16[1536,2048]{1,0:T(8,128)(2,1)} %get-tuple-element.89.x_ref, f32[1,2048]{1,0:T(1,128)S(1)} %bitcast.56, bf16[2048,1536]{1,0:T(8,128)(2,1)} %bitcast.59), custom_call_target="tpu_custom_call" | custom-call | flops 150994944 | bytes 172032 | tf_op jit(solution)/shard_map/project/pallas_call | solution.py:895
  241.9 3.0 collective-permute-start.1
  246.6 2.8 fusion.10
  252.9 2.5 turn.1
  257.7 21.7 %attend.1 = (bf16[1536,512]{1,0:T(8,128)(2,1)}, f32[4,1,1536]{2,1,0:T(1,128)}) custom-call(bf16[1536,512]{1,0:T(8,128)(2,1)} %copy-done.6, bf16[1536,512]{1,0:T(8,128)(2,1)} %copy-done.7, bf16[1536,512]{1,0:T(8,128)(2,1)} %copy-done.5, s32[1,1536]{1,0:T(1,128)} %broadcast_in_dim.20.start_ref, s32[1,1536]{1,0:T(1,128)} %broadcast_in_dim.21.place_ref, ...), custom_call_target="tpu_custom_call" | custom-call | flops 301989888 | bytes 98304 | tf_op jit(solution)/shard_map/attend/pallas_call | solution.py:1059
  279.4 5.1 convolution_convert_fusion
  284.5 3.3 fusion.19
  287.7 4.4 all-gather.2.cloned.1.call-done.rows_ref.cb_ref
  292.1 1.9 copy-done.3
  294.0 6.5 dispatch.4.rows_ref
  300.5 86.1 %hide.2 = (f32[768,2048]{1,0:T(8,128)}, bf16[768,2048]{1,0:T(8,128)(2,1)}, bf16[8,2,224,1024]{3,2,1,0:T(8,128)(2,1)}) custom-call(bf16[768,2048]{1,0:T(8,128)(2,1)} %get-tuple-element.206.p_ref, bf16[1536,2048]{1,0:T(8,128)(2,1)} %get-tuple-element.89.x_ref, f32[1,2048]{1,0:T(1,128)} %bitcast.62, bf16[8,2,224,1024]{3,2,1,0:T(8,128)(2,1)} %dispatch.4.rows_ref), custom_call_target="tpu_custom_call" | custom-call | bytes 4915200 | tf_op jit(solution)/shard_map/hide/pallas_call | solution.py:394
  388.5 6.3 dispatch.5.rows_ref
  394.8 85.9 %hide.3 = (f32[768,2048]{1,0:T(8,128)}, bf16[768,2048]{1,0:T(8,128)(2,1)}, bf16[8,2,112,2048]{3,2,1,0:T(8,128)(2,1)}) custom-call(bf16[768,2048]{1,0:T(8,128)(2,1)} %get-tuple-element.207.p_ref, bf16[1536,2048]{1,0:T(8,128)(2,1)} %get-tuple-element.89.x_ref, f32[1,2048]{1,0:T(1,128)} %bitcast.63, bf16[8,2,112,2048]{3,2,1,0:T(8,128)(2,1)} %dispatch.5.rows_ref), custom_call_target="tpu_custom_call" | custom-call | bytes 4915200 | tf_op jit(solution)/shard_map/hide/pallas_call | solution.py:394
  480.7 1.9 copy-done.12
  482.6 6.3 dispatch.6
  488.9 4.9 all-to-all-start.1
  495.7 75.9 %experts.2 = (bf16[8,2,224,2048]{3,2,1,0:T(8,128)(2,1)}, bf16[8,2,112,2048]{3,2,1,0:T(8,128)(2,1)}, bf16[4,896,512]{2,1,0:T(8,128)(2,1)}, bf16[4,896,512]{2,1,0:...) custom-call(bf16[8,2,112,2048]{3,2,1,0:T(8,128)(2,1)} %get-tuple-element.107.x_ref.x0_ref, ...), custom_call_target="tpu_custom_call" | custom-call | flops 704643072 | bytes 573440 | tf_op jit(solution)/shard_map/experts/pallas_call | solution.py:1330
  571.6 4.9 all-to-all-done.1.x_ref.x1_ref
  576.6 4.9 all-to-all-start.2
  581.4 76.3 %experts.3 = (bf16[8,2,224,2048]{3,2,1,0:T(8,128)(2,1)}, bf16[8,2,112,2048]{3,2,1,0:T(8,128)(2,1)}, bf16[4,896,512]{2,1,0:T(8,128)(2,1)}, bf16[4,896,512]{2,1,0:...) custom-call(bf16[8,2,112,2048]{3,2,1,0:T(8,128)(2,1)} %all-to-all-done.1, ...), custom_call_target="tpu_custom_call", output_to_operand_aliasing={{0}: (8, {})} | custom-call | flops 704643072 | bytes 573440 | tf_op jit(solution)/shard_map/experts/pallas_call | solution.py:1330
  657.8 6.5 all-to-all-done.2.rows_ref
  664.3 5.0 all-to-all-start.3
  670.4 9.8 combine.3.p_ref
  680.2 84.7 %hide_back.2 = (f32[768,2048]{1,0:T(8,128)}, bf16[768,2048]{1,0:T(8,128)(2,1)}, f32[1,2048]{1,0:T(1,128)}) custom-call(bf16[768,2048]{1,0:T(8,128)(2,1)} %combine.3.p_ref, f32[768,2048]{1,0:T(8,128)} %get-tuple-element.99.hidden_ref, bf16[1536,1024]{1,0:T(8,128)(2,1)} %get-tuple-element.103.rows_ref.ca_ref, ...), custom_call_target="tpu_custom_call" | custom-call | bytes 4259840 | tf_op jit(solution)/shard_map/hide_back/pallas_call | solution.py:465
  765.0 5.6 all-to-all-start.4
  770.6 5.2 convolution_convert_fusion.2
  775.8 9.8 combine.4.p_ref
  785.6 84.8 %hide_back.3 = (f32[768,2048]{1,0:T(8,128)}, bf16[768,2048]{1,0:T(8,128)(2,1)}, f32[1,2048]{1,0:T(1,128)}) custom-call(bf16[768,2048]{1,0:T(8,128)(2,1)} %combine.4.p_ref, f32[768,2048]{1,0:T(8,128)} %get-tuple-element.101.hidden_ref, bf16[1536,1024]{1,0:T(8,128)(2,1)} %get-tuple-element.103.rows_ref.ca_ref, ...), custom_call_target="tpu_custom_call" | custom-call | bytes 4259840 | tf_op jit(solution)/shard_map/hide_back/pallas_call | solution.py:465
  870.4 4.4 convolution_convert_fusion.1
  876.1 37.6 %attend_back.1 = (bf16[1536,512]{1,0:T(8,128)(2,1)}, bf16[1536,512]{1,0:T(8,128)(2,1)}, bf16[1536,512]{1,0:T(8,128)(2,1)}) custom-call(bf16[1536,512]{1,0:T(8,128)(2,1)} %copy-done.6, bf16[1536,512]{1,0:T(8,128)(2,1)} %copy-done.7, bf16[1536,512]{1,0:T(8,128)(2,1)} %copy-done.5, bf16[1536,512]{1,0:T(8,128)(2,1)} %pad_maximum_fusion.g_ref, ...), custom_call_target="tpu_custom_call" | custom-call | flops 566231040 | bytes 196608 | tf_op jit(solution)/shard_map/attend_back/pallas_call | solution.py:1117
  913.7 2.8 copy-done.1
  919.3 5.6 turn_back.1
  924.9 7.1 all-to-all-done.4.rows_ref
  932.0 17.8 %combine.5 = bf16[1536,2048]{1,0:T(8,128)(2,1)} custom-call(bf16[2,768,16]{2,1,0:T(8,128)(2,1)} %copy-done.17, bf16[8,2,224,2048]{3,2,1,0:T(8,128)(2,1)} %all-to-all-done.4.rows_ref), custom_call_target="tpu_custom_call" | custom-call | flops 176160768 | bytes 229376 | tf_op jit(solution)/shard_map/combine/pallas_call | solution.py:1256
  950.8 3.0 collective-permute-start.5
  956.4 27.6 %down_grad.1 = f32[4,512,2048]{2,1,0:T(8,128)} custom-call(bf16[4,896,512]{2,1,0:T(8,128)(2,1)} %get-tuple-element.143.a0_ref, bf16[4,896,512]{2,1,0:T(8,128)(2,1)} %get-tuple-element.144.a1_ref, bf16[8,2,224,1024]{3,2,1,0:T(8,128)(2,1)} %all-to-all-done.ca_ref.kept_ref, bf16[8,2,224,1024]{3,2,1,0:T(8,128)(2,1)} %get-tuple-element.106.cb_ref), custom_call_target="tpu_custom_call" | custom-call | flops 234881024 | bytes 262144 | tf_op jit(solution)/shard_map/down_grad/pallas_call | solution.py:1412
  984.0 47.2 %wide_grad.1 = (f32[4,2048,512]{2,1,0:T(8,128)}, f32[4,2048,512]{2,1,0:T(8,128)}, f32[2,2048,64]{2,1,0:T(8,128)}) custom-call(bf16[8,2,112,2048]{3,2,1,0:T(8,128)(2,1)} %get-tuple-element.107.x_ref.x0_ref, bf16[8,2,112,2048]{3,2,1,0:T(8,128)(2,1)} %all-to-all-done.1.x_ref.x1_ref, bf16[4,896,512]{2,1,0:T(8,128)(2,1)} %get-tuple-element.135.g0_ref, ...), custom_call_target="tpu_custom_call" | custom-call | flops 469762048 | bytes 524288 | tf_op jit(solution)/shard_map/wide_grad/pallas_call | solution.py:1376
  1031.2 2.2 reduce_sum.29
  1037.1 17.1 %join_slopes.1 = (bf16[1536,1536]{1,0:T(8,128)(2,1)}, bf16[1536,2048]{1,0:T(8,128)(2,1)}) custom-call(bf16[1536,512]{1,0:T(8,128)(2,1)S(1)} %copy-done.9, bf16[1536,512]{1,0:T(8,128)(2,1)S(1)} %copy-done.11, bf16[1536,512]{1,0:T(8,128)(2,1)} %get-tuple-element.125.dv_ref, f32[1536,1024]{1,0:T(8,128)} %get-tuple-element.92.raw_ref, ...), custom_call_target="tpu_custom_call" | custom-call | flops 150994944 | bytes 393216 | tf_op jit(solution)/shard_map/join_slopes/pallas_call | solution.py:1017
  1054.2 15.0 %joint_grad.1 = bf16[2048,1664]{1,0:T(8,128)(2,1)} custom-call(bf16[1536,2048]{1,0:T(8,128)(2,1)} %get-tuple-element.147.normed_ref, bf16[1536,1536]{1,0:T(8,128)(2,1)} %get-tuple-element.148.joint_ref, bf16[2048,128]{1,0:T(8,128)(2,1)} %pad.4.router_ref), custom_call_target="tpu_custom_call" | custom-call | flops 150994944 | bytes 294912 | tf_op jit(solution)/shard_map/joint_grad/pallas_call | solution.py:1179
  1071.1 3.2 add_convert_fusion
  1074.2 138.8 %finish.1 = (bf16[384,2048]{1,0:T(8,128)(2,1)}, bf16[4,8,64,1664]{3,2,1,0:T(8,128)(2,1)}, bf16[8,64,2048]{2,1,0:T(8,128)(2,1)}, f32[8,512]{1,0:T(8,128)}) custom-call(bf16[1536,2048]{1,0:T(8,128)(2,1)} %get-tuple-element.146.p_ref, bf16[4,4,2,64,1664]{4,3,2,1,0:T(8,128)(2,1)} %bitcast.58, bf16[4,2,64,2048]{3,2,1,0:T(8,128)(2,1)} %bitcast.61, ...), custom_call_target="tpu_custom_call" | custom-call | bytes 6553600 | tf_op jit(solution)/shard_map/finish/pallas_call | solution.py:823
  1213.0 2.9 copy-done.4
  1217.6 6.4 widen.1
  1225.4 5.4 add_convert_fusion.1
  (145 shorter events, 47.0 us)
Async XLA Ops:
  8.7 4.4 copy-start.24
  9.7 3.7 copy-start.25
  9.7 4.0 copy-start.27
  9.7 4.0 copy-start.28
  204.2 8.3 copy-start.2
  219.1 5.0 copy-start.16
  219.1 269.7 %all-to-all-start = ((bf16[8,2,224,1024]{3,2,1,0:T(8,128)(2,1)}), bf16[8,2,224,1024]{3,2,1,0:T(8,128)(2,1)}, u32[]{:S(2)}, u32[]{:S(2)}) async-start(bf16[8,2,224,1024]{3,2,1,0:T(8,128)(2,1)} %dispatch.7), calls=%async_computation | async-start | bytes 14680064 | tf_op jit(solution)/shard_map/all_to_all | solution.py:856
  224.1 68.0 %all-gather.2.cloned.1.call-start = ((), (), s32[]{:S(2)}) async-start(), calls=%async_computation.6 | async-start | bytes 3932160 | tf_op jit(solution)/shard_map/all_gather | solution.py:1488
  225.2 15.6 %copy-start.15 = (f32[1,1,4,512]{3,1,2,0:T(1,128)}, f32[1,1,4,512]{3,1,2,0:T(1,128)S(1)}, u32[]{:S(2)}) copy-start(f32[1,1,4,512]{3,1,2,0:T(1,128)S(1)} %copy.58) | copy-start | bytes 24580
  225.2 21.0 %copy-start.31 = (s32[1,2]{1,0:T(1,128)S(1)}, s32[1,2]{1,0:T(1,128)}, u32[]{:S(2)}) copy-start(s32[1,2]{1,0:T(1,128)} %param.31) | copy-start | bytes 28
  225.2 21.2 %copy-start.29 = (bf16[512]{0:T(512)(128)(2,1)S(1)}, bf16[512]{0:T(512)(128)(2,1)}, u32[]{:S(2)}) copy-start(bf16[512]{0:T(512)(128)(2,1)} %param.24) | copy-start | bytes 3076
  225.2 21.2 %copy-start.30 = (bf16[512]{0:T(512)(128)(2,1)S(1)}, bf16[512]{0:T(512)(128)(2,1)}, u32[]{:S(2)}) copy-start(bf16[512]{0:T(512)(128)(2,1)} %param.25) | copy-start | bytes 3076
  225.2 21.2 %copy-start.23 = (s32[1536]{0:T(1024)S(1)}, s32[1536]{0:T(1024)}, u32[]{:S(2)}) copy-start(s32[1536]{0:T(1024)} %param.32) | copy-start | bytes 18436
  240.8 1.2 copy-start.5
  241.9 10.9 collective-permute-start
  241.9 10.9 collective-permute-start.1
  245.0 7.9 collective-permute-start.2
  246.5 6.3 copy-start
  255.4 1.1 copy-start.6
  256.5 1.1 copy-start.7
  257.7 21.7 %copy-start.33 = (bf16[512,2048]{1,0:T(8,128)(2,1)S(1)}, bf16[512,2048]{1,0:T(8,128)(2,1)}, u32[]{:S(2)}) copy-start(bf16[512,2048]{1,0:T(8,128)(2,1)} %param.21) | copy-start | bytes 6291460
  292.1 1.9 copy-start.3
  386.6 1.9 copy-start.13
  480.7 1.9 copy-start.12
  488.9 87.7 %all-to-all-start.1 = ((bf16[8,2,112,2048]{3,2,1,0:T(8,128)(2,1)}), bf16[8,2,112,2048]{3,2,1,0:T(8,128)(2,1)}, u32[]{:S(2)}, u32[]{:S(2)}) async-start(bf16[8,2,112,2048]{3,2,1,0:T(8,128)(2,1)} %dispatch.6), calls=%async_computation.1 | async-start | bytes 14680064 | tf_op jit(solution)/shard_map/all_to_all | solution.py:856
  576.6 87.7 %all-to-all-start.2 = ((bf16[8,2,112,2048]{3,2,1,0:T(8,128)(2,1)}), bf16[8,2,112,2048]{3,2,1,0:T(8,128)(2,1)}, u32[]{:S(2)}, u32[]{:S(2)}) async-start(bf16[8,2,112,2048]{3,2,1,0:T(8,128)(2,1)} %get-tuple-element.112), calls=%async_computation.2 | async-start | bytes 14680064 | tf_op jit(solution)/shard_map/all_to_all | solution.py:856
  664.3 5.0 copy-start.20
  664.3 100.7 %all-to-all-start.3 = ((bf16[8,2,112,2048]{3,2,1,0:T(8,128)(2,1)}), bf16[8,2,112,2048]{3,2,1,0:T(8,128)(2,1)}, u32[]{:S(2)}, u32[]{:S(2)}) async-start(bf16[8,2,112,2048]{3,2,1,0:T(8,128)(2,1)} %get-tuple-element.113), calls=%async_computation.3 | async-start | bytes 14680064 | tf_op jit(solution)/shard_map/all_to_all | solution.py:856
  669.5 10.7 copy-start.17
  765.0 167.1 %all-to-all-start.4 = ((bf16[8,2,224,2048]{3,2,1,0:T(8,128)(2,1)}), bf16[8,2,224,2048]{3,2,1,0:T(8,128)(2,1)}, u32[]{:S(2)}, u32[]{:S(2)}) async-start(bf16[8,2,224,2048]{3,2,1,0:T(8,128)(2,1)} %get-tuple-element.117), calls=%async_computation.4 | async-start | bytes 29360128 | tf_op jit(solution)/shard_map/all_to_all | solution.py:856
  770.5 454.8 %reduce-scatter.2.cloned.1.call-start = ((), (), s32[]{:S(2)}) async-start(), calls=%async_computation.7 | async-start | bytes 7864320 | tf_op jit(solution)/shard_map/reduce_scatter | solution.py:1585
  870.4 4.4 copy-start.21
  913.7 2.8 copy-start.1
  916.5 1.4 copy-start.8
  917.9 1.4 copy-start.10
  950.0 6.4 collective-permute-start.3
  950.0 6.4 collective-permute-start.4
  950.8 5.6 collective-permute-start.5
  1034.3 1.4 copy-start.9
  1035.7 1.4 copy-start.11
  1054.2 15.0 %copy-start.18 = (bf16[768,2048]{1,0:T(8,128)(2,1)S(1)}, bf16[768,2048]{1,0:T(8,128)(2,1)}, u32[]{:S(2)}) copy-start(bf16[768,2048]{1,0:T(8,128)(2,1)} %get-tuple-element.150) | copy-start | bytes 9437188
  1054.2 15.0 %copy-start.22 = (bf16[1536,512]{1,0:T(8,128)(2,1)S(1)}, bf16[1536,512]{1,0:T(8,128)(2,1)}, u32[]{:S(2)}) copy-start(bf16[1536,512]{1,0:T(8,128)(2,1)} %get-tuple-element.97) | copy-start | bytes 4718596
  1069.2 1.9 copy-start.32
  1213.0 2.9 copy-start.4
  1216.0 1.6 copy-start.14
  1217.6 7.2 copy-start.26
  1225.4 5.4 copy-start.19
Sparse Core Ops, SparseCore 0:
  227.1 64.9 all-gather.1
  950.0 107.4 reduce-scatter.1

commit v3 on v2

--- a/solution.py
+++ b/solution.py
@@ -890,7 +890,7 @@
 
 def project(block, gain, columns, tile):
     group, width = block.shape
-    own = columns.shape[1] // 3
+    own = columns.shape[1] // 3 // 128 * 128
     rows = lambda count: pl.BlockSpec((tile, count), lambda i: (i, 0))
     return pl.pallas_call(
         project_kernel,
@@ -1389,6 +1389,15 @@
     )(*xs, *gslopes, *uslopes, *logit_slopes)
 
 
+def down_grad_unit_kernel(a0_ref, a1_ref, ca_ref, cb_ref, d_ref):
+    half, slots = ca_ref.shape[-1], ca_ref.shape[2] // 2
+    a0, a1 = a0_ref[0].T, a1_ref[0].T
+    for which, c_ref in enumerate((ca_ref, cb_ref)):
+        d_ref[0, :, which * half:(which + 1) * half] = dot(
+            a0, c_ref[:, :, :slots].reshape(-1, half)
+        ) + dot(a1, c_ref[:, :, slots:].reshape(-1, half))
+
+
 def down_grad_kernel(a0_ref, a1_ref, ca_ref, cb_ref, d_ref):
     tile, slots = ca_ref.shape[-1], ca_ref.shape[2] // 2
 
@@ -1405,7 +1414,20 @@
 def down_grad(acts, cs, halves):
     planes, local, double, half = cs[0].shape
     units, count, hidden = acts[0].shape
-    tile = half if planes * double <= 2048 else 512
+    if planes * double <= 2048:
+        a_spec = pl.BlockSpec((1, count, hidden), lambda u: (u, 0, 0))
+        c_spec = pl.BlockSpec((planes, 1, double, half), lambda u: (0, u // halves, 0, 0))
+        return pl.pallas_call(
+            down_grad_unit_kernel,
+            grid=(units,),
+            out_shape=shape_of((units, hidden, 2 * half), F32),
+            in_specs=[a_spec, a_spec, c_spec, c_spec],
+            out_specs=pl.BlockSpec((1, hidden, 2 * half), lambda u: (u, 0, 0)),
+            compiler_params=params(60),
+            cost_estimate=cost(8 * units * count * hidden * half, 8 * units * hidden * half),
+            name="down_grad",
+        )(*acts, *cs)
+    tile = 512
     steps = half // tile
     a_spec = pl.BlockSpec((1, count, hidden), lambda u, j: (u, 0, 0))
     shape = (planes, 1, double, tile)
@@ -1466,22 +1488,29 @@
 
     sent = jnp.stack([own_slice(w) for w in (query_weight, key_weight, value_weight)], axis=1)
     sent = jnp.moveaxis(sent.reshape(slice_rows, 3, line, own_width), 2, 0)
-    sent = sent.reshape(line, slice_rows, 3 * own_width)
+    routing = jnp.pad(own_slice(router_weight), ((0, 0), (0, -expert_count % 128)))
+    sent = jnp.concatenate(
+        [
+            sent.reshape(line, slice_rows, 3 * own_width),
+            jnp.broadcast_to(routing, (line,) + routing.shape),
+        ],
+        axis=2,
+    )
     top_count = routes.shape[1]
-    packed = [router_weight, first_gain, second_gain, routes.astype(BF)]
+    packed = [first_gain, second_gain, routes.astype(BF)]
     sizes = [array.size for array in packed]
     fill = -sum(sizes) % (16 * 128)
     small = jnp.concatenate([array.reshape(-1) for array in packed] + [jnp.zeros((fill,), BF)])
     block_in, first_half, small_all, columns, _ = gather_start(
         inputs, cotangent, small.reshape(-1, 128), sent, planes, line
     )
-    columns = columns.reshape(width, 3 * own_width)
+    columns = columns.reshape(width, -1)
+    full_router = columns[:, 3 * own_width:3 * own_width + expert_count]
     small_all = small_all.reshape(line, -1)
-    ends = [sum(sizes[:i]) for i in range(5)]
-    full_router, gain_first, gain_second, routes_all = (
-        small_all[:, ends[i]:ends[i + 1]] for i in range(4)
-    )
-    full_router = full_router.reshape(width, expert_count)
+    ends = [sum(sizes[:i]) for i in range(4)]
+    gain_first, gain_second, routes_all = (
+        small_all[:, ends[i]:ends[i + 1]] for i in range(3)
+    )
     gain_first, gain_second = (g.reshape(width).astype(F32) for g in (gain_first, gain_second))
     routes_all = routes_all.reshape(line, tokens, top_count).astype(jnp.int32)
     later, _ = lax.optimization_barrier((cotangent, block_in))

time: 1250 us -> 1240 us (level)
  no operation moved by 1% of the time
where the time goes in v3:
time: 1240 us; the launch traced here: 1230 us
  Pallas kernels  1080 us (87%)
  local copies, waits for them, and re-layouts  45 us (4%)
  starting transfers between devices  33.1 us (3%)
  waiting for transfers between devices  21.7 us (2%)
  matrix products  21.2 us (2%)
  other arithmetic  18.5 us (1%)
  between operations  15 us (1%)
    pallas_call x1, Pallas kernels, gather_start(): pl.pallas_call(functools.partial(gather_kernel, planes, line, pieces), ou...  188 us
    pallas_call x2, Pallas kernels, hide(): pl.pallas_call(functools.partial(hide_kernel, planes, line, pieces, lag,...  172 us
    pallas_call x2, Pallas kernels, hide_back(): pl.pallas_call(functools.partial(hide_back_kernel, line, pieces, lag, at)...  169 us
    pallas_call x2, Pallas kernels, experts(): pl.pallas_call(functools.partial(expert_kernel, halves), grid=(local, ste...  152 us
    pallas_call x1, Pallas kernels, finish(): pl.pallas_call(functools.partial(finish_kernel, planes, line, height, lag...  139 us
    pallas_call x1, Pallas kernels, wide_grad(): pl.pallas_call(wide_grad_kernel, grid=(local, width // tile), out_shape=(...  47.2 us
    pallas_call x1, Pallas kernels, attend_back(): pl.pallas_call(functools.partial(attend_back_kernel, size), grid=(heads /...  37.6 us
    pallas_call x3, Pallas kernels, combine(): pl.pallas_call(functools.partial(combine_kernel, slots), grid=(chunks, wi...  37.5 us
  transfers between devices with their start and end apart: 13, of which 4 were waited for; matrix products, arithmetic and copies ran while one was open for 3% of the time, Pallas kernels for 70%

profile of v3, /device:TPU:0, one launch (start us, length us, event | category | flops | bytes accessed | tf_op | source)
XLA Modules:
  0.0 1232.8 jit_solution(11379698454869089386)
XLA Ops:
  14.5 188.4 %gather_start.1 = (bf16[1536,2048]{1,0:T(8,128)(2,1)}, bf16[1536,1024]{1,0:T(8,128)(2,1)}, bf16[128,128]{1,0:T(8,128)(2,1)}, bf16[4,8,64,1664]{3,2,1,0:T(8,128)(2,1)}, bf16[4,64,1664]{2,1,0:T(8,128)(2,1)}) custom-call(bf16[384,2048]{1,0:T(8,128)(2,1)} %x_ref.3, bf16[384,2048]{1,0:T(8,128)(2,1)} %c_ref.1, bf16[32,128]{1,0:T(8,128)(2,1)} %maximum_bitcast_fusion.1.small_ref, ...), custom_call_target="tpu_custom_call" | custom-call | tf_op jit(solution)/shard_map/gather_start/pallas_call | solution.py:192
  209.4 6.6 dispatch.7
  216.0 5.0 all-to-all-start
  222.1 16.2 %project.1 = (bf16[1536,2048]{1,0:T(8,128)(2,1)}, f32[1536,1024]{1,0:T(8,128)}, bf16[1536,512]{1,0:T(8,128)(2,1)S(1)}, f32[2,1536]{1,0:T(2,128)S(1)}) custom-call(bf16[1536,2048]{1,0:T(8,128)(2,1)} %get-tuple-element.89.x_ref, f32[1,2048]{1,0:T(1,128)S(1)} %bitcast.56, bf16[2048,1664]{1,0:T(8,128)(2,1)} %bitcast.58), custom_call_target="tpu_custom_call" | custom-call | flops 150994944 | bytes 172032 | tf_op jit(solution)/shard_map/project/pallas_call | solution.py:895
  239.5 3.0 collective-permute-start.1
  243.9 2.8 fusion.10
  250.2 2.5 turn.1
  255.0 21.7 %attend.1 = (bf16[1536,512]{1,0:T(8,128)(2,1)}, f32[4,1,1536]{2,1,0:T(1,128)}) custom-call(bf16[1536,512]{1,0:T(8,128)(2,1)} %copy-done.8, bf16[1536,512]{1,0:T(8,128)(2,1)} %copy-done.9, bf16[1536,512]{1,0:T(8,128)(2,1)} %copy-done.7, s32[1,1536]{1,0:T(1,128)} %broadcast_in_dim.23.start_ref, s32[1,1536]{1,0:T(1,128)} %broadcast_in_dim.24.place_ref, ...), custom_call_target="tpu_custom_call" | custom-call | flops 301989888 | bytes 98304 | tf_op jit(solution)/shard_map/attend/pallas_call | solution.py:1059
  276.7 5.1 convolution_convert_fusion
  281.7 3.3 fusion.20
  285.0 4.0 all-gather.2.cloned.1.call-done.rows_ref.cb_ref
  289.0 1.9 copy-done.5
  290.9 6.5 dispatch.4.rows_ref
  297.4 86.1 %hide.2 = (f32[768,2048]{1,0:T(8,128)}, bf16[768,2048]{1,0:T(8,128)(2,1)}, bf16[8,2,224,1024]{3,2,1,0:T(8,128)(2,1)}) custom-call(bf16[768,2048]{1,0:T(8,128)(2,1)} %get-tuple-element.206.p_ref, bf16[1536,2048]{1,0:T(8,128)(2,1)} %get-tuple-element.89.x_ref, f32[1,2048]{1,0:T(1,128)} %bitcast.63, bf16[8,2,224,1024]{3,2,1,0:T(8,128)(2,1)} %dispatch.4.rows_ref), custom_call_target="tpu_custom_call" | custom-call | bytes 4915200 | tf_op jit(solution)/shard_map/hide/pallas_call | solution.py:394
  383.5 1.9 copy-done.15
  385.4 6.3 dispatch.5.rows_ref
  391.7 85.9 %hide.3 = (f32[768,2048]{1,0:T(8,128)}, bf16[768,2048]{1,0:T(8,128)(2,1)}, bf16[8,2,112,2048]{3,2,1,0:T(8,128)(2,1)}) custom-call(bf16[768,2048]{1,0:T(8,128)(2,1)} %get-tuple-element.207.p_ref, bf16[1536,2048]{1,0:T(8,128)(2,1)} %get-tuple-element.89.x_ref, f32[1,2048]{1,0:T(1,128)} %bitcast.64, bf16[8,2,112,2048]{3,2,1,0:T(8,128)(2,1)} %dispatch.5.rows_ref), custom_call_target="tpu_custom_call" | custom-call | bytes 4915200 | tf_op jit(solution)/shard_map/hide/pallas_call | solution.py:394
  479.4 6.3 dispatch.6
  485.7 4.8 all-to-all-start.1
  493.1 76.2 %experts.2 = (bf16[8,2,224,2048]{3,2,1,0:T(8,128)(2,1)}, bf16[8,2,112,2048]{3,2,1,0:T(8,128)(2,1)}, bf16[4,896,512]{2,1,0:T(8,128)(2,1)}, bf16[4,896,512]{2,1,0:...) custom-call(bf16[8,2,112,2048]{3,2,1,0:T(8,128)(2,1)} %get-tuple-element.107.x_ref.x0_ref, ...), custom_call_target="tpu_custom_call" | custom-call | flops 704643072 | bytes 573440 | tf_op jit(solution)/shard_map/experts/pallas_call | solution.py:1330
  569.2 4.1 all-to-all-done.1.x_ref.x1_ref
  573.4 4.9 all-to-all-start.2
  578.3 76.3 %experts.3 = (bf16[8,2,224,2048]{3,2,1,0:T(8,128)(2,1)}, bf16[8,2,112,2048]{3,2,1,0:T(8,128)(2,1)}, bf16[4,896,512]{2,1,0:T(8,128)(2,1)}, bf16[4,896,512]{2,1,0:...) custom-call(bf16[8,2,112,2048]{3,2,1,0:T(8,128)(2,1)} %all-to-all-done.1, ...), custom_call_target="tpu_custom_call", output_to_operand_aliasing={{0}: (8, {})} | custom-call | flops 704643072 | bytes 573440 | tf_op jit(solution)/shard_map/experts/pallas_call | solution.py:1330
  654.6 6.5 all-to-all-done.2.rows_ref
  661.1 5.0 all-to-all-start.3
  667.2 9.8 combine.3.p_ref
  677.0 84.7 %hide_back.2 = (f32[768,2048]{1,0:T(8,128)}, bf16[768,2048]{1,0:T(8,128)(2,1)}, f32[1,2048]{1,0:T(1,128)}) custom-call(bf16[768,2048]{1,0:T(8,128)(2,1)} %combine.3.p_ref, f32[768,2048]{1,0:T(8,128)} %get-tuple-element.99.hidden_ref, bf16[1536,1024]{1,0:T(8,128)(2,1)} %get-tuple-element.103.rows_ref.ca_ref, ...), custom_call_target="tpu_custom_call" | custom-call | bytes 4259840 | tf_op jit(solution)/shard_map/hide_back/pallas_call | solution.py:465
  761.8 5.6 all-to-all-start.4
  767.4 5.2 convolution_convert_fusion.2
  772.6 9.8 combine.4.p_ref
  782.5 84.7 %hide_back.3 = (f32[768,2048]{1,0:T(8,128)}, bf16[768,2048]{1,0:T(8,128)(2,1)}, f32[1,2048]{1,0:T(1,128)}) custom-call(bf16[768,2048]{1,0:T(8,128)(2,1)} %combine.4.p_ref, f32[768,2048]{1,0:T(8,128)} %get-tuple-element.101.hidden_ref, bf16[1536,1024]{1,0:T(8,128)(2,1)} %get-tuple-element.103.rows_ref.ca_ref, ...), custom_call_target="tpu_custom_call" | custom-call | bytes 4259840 | tf_op jit(solution)/shard_map/hide_back/pallas_call | solution.py:465
  867.2 4.4 convolution_convert_fusion.1
  872.9 37.6 %attend_back.1 = (bf16[1536,512]{1,0:T(8,128)(2,1)}, bf16[1536,512]{1,0:T(8,128)(2,1)}, bf16[1536,512]{1,0:T(8,128)(2,1)}) custom-call(bf16[1536,512]{1,0:T(8,128)(2,1)} %copy-done.8, bf16[1536,512]{1,0:T(8,128)(2,1)} %copy-done.9, bf16[1536,512]{1,0:T(8,128)(2,1)} %copy-done.7, bf16[1536,512]{1,0:T(8,128)(2,1)} %pad_maximum_fusion.g_ref, ...), custom_call_target="tpu_custom_call" | custom-call | flops 566231040 | bytes 196608 | tf_op jit(solution)/shard_map/attend_back/pallas_call | solution.py:1117
  910.6 2.8 copy-done.3
  916.2 5.6 turn_back.1
  921.8 7.1 all-to-all-done.4.rows_ref
  928.8 17.8 %combine.5 = bf16[1536,2048]{1,0:T(8,128)(2,1)} custom-call(bf16[2,768,16]{2,1,0:T(8,128)(2,1)} %copy-done.19, bf16[8,2,224,2048]{3,2,1,0:T(8,128)(2,1)} %all-to-all-done.4.rows_ref), custom_call_target="tpu_custom_call" | custom-call | flops 176160768 | bytes 229376 | tf_op jit(solution)/shard_map/combine/pallas_call | solution.py:1256
  947.6 3.0 collective-permute-start.5
  953.2 24.7 %down_grad.1 = f32[4,512,2048]{2,1,0:T(8,128)} custom-call(bf16[4,896,512]{2,1,0:T(8,128)(2,1)} %get-tuple-element.143.a0_ref, bf16[4,896,512]{2,1,0:T(8,128)(2,1)} %get-tuple-element.144.a1_ref, bf16[8,2,224,1024]{3,2,1,0:T(8,128)(2,1)} %all-to-all-done.ca_ref.kept_ref, bf16[8,2,224,1024]{3,2,1,0:T(8,128)(2,1)} %get-tuple-element.106.cb_ref), custom_call_target="tpu_custom_call" | custom-call | flops 234881024 | bytes 262144 | tf_op jit(solution)/shard_map/down_grad/pallas_call | solution.py:1420
  977.9 47.2 %wide_grad.1 = (f32[4,2048,512]{2,1,0:T(8,128)}, f32[4,2048,512]{2,1,0:T(8,128)}, f32[2,2048,64]{2,1,0:T(8,128)}) custom-call(bf16[8,2,112,2048]{3,2,1,0:T(8,128)(2,1)} %get-tuple-element.107.x_ref.x0_ref, bf16[8,2,112,2048]{3,2,1,0:T(8,128)(2,1)} %all-to-all-done.1.x_ref.x1_ref, bf16[4,896,512]{2,1,0:T(8,128)(2,1)} %get-tuple-element.135.g0_ref, ...), custom_call_target="tpu_custom_call" | custom-call | flops 469762048 | bytes 524288 | tf_op jit(solution)/shard_map/wide_grad/pallas_call | solution.py:1376
  1025.2 2.1 reduce_sum.29
  1031.0 17.0 %join_slopes.1 = (bf16[1536,1536]{1,0:T(8,128)(2,1)}, bf16[1536,2048]{1,0:T(8,128)(2,1)}) custom-call(bf16[1536,512]{1,0:T(8,128)(2,1)S(1)} %copy-done.11, bf16[1536,512]{1,0:T(8,128)(2,1)S(1)} %copy-done.13, bf16[1536,512]{1,0:T(8,128)(2,1)} %get-tuple-element.125.dv_ref, f32[1536,1024]{1,0:T(8,128)} %get-tuple-element.92.raw_ref, ...), custom_call_target="tpu_custom_call" | custom-call | flops 150994944 | bytes 393216 | tf_op jit(solution)/shard_map/join_slopes/pallas_call | solution.py:1017
  1048.0 15.0 %joint_grad.1 = bf16[2048,1664]{1,0:T(8,128)(2,1)} custom-call(bf16[1536,2048]{1,0:T(8,128)(2,1)} %get-tuple-element.147.normed_ref, bf16[1536,1536]{1,0:T(8,128)(2,1)} %get-tuple-element.148.joint_ref, bf16[2048,128]{1,0:T(8,128)(2,1)} %pad.9.router_ref), custom_call_target="tpu_custom_call" | custom-call | flops 150994944 | bytes 294912 | tf_op jit(solution)/shard_map/joint_grad/pallas_call | solution.py:1179
  1064.9 3.2 add_convert_fusion
  1068.0 138.8 %finish.1 = (bf16[384,2048]{1,0:T(8,128)(2,1)}, bf16[4,8,64,1664]{3,2,1,0:T(8,128)(2,1)}, bf16[8,64,2048]{2,1,0:T(8,128)(2,1)}, f32[8,512]{1,0:T(8,128)}) custom-call(bf16[1536,2048]{1,0:T(8,128)(2,1)} %get-tuple-element.146.p_ref, bf16[4,4,2,64,1664]{4,3,2,1,0:T(8,128)(2,1)} %bitcast.61, bf16[4,2,64,2048]{3,2,1,0:T(8,128)(2,1)} %bitcast.62, ...), custom_call_target="tpu_custom_call" | custom-call | bytes 6553600 | tf_op jit(solution)/shard_map/finish/pallas_call | solution.py:823
  1206.8 2.9 copy-done.6
  1211.4 6.4 widen.1
  1219.2 5.4 add_convert_fusion.1
  (151 shorter events, 45.7 us)
Async XLA Ops:
  7.2 5.1 copy-start
  8.7 3.8 copy-start.27
  10.5 3.3 copy-start.29
  10.5 3.3 copy-start.30
  202.9 6.5 copy-start.4
  209.4 6.6 copy-start.22
  216.0 5.0 copy-start.18
  216.0 269.7 %all-to-all-start = ((bf16[8,2,224,1024]{3,2,1,0:T(8,128)(2,1)}), bf16[8,2,224,1024]{3,2,1,0:T(8,128)(2,1)}, u32[]{:S(2)}, u32[]{:S(2)}) async-start(bf16[8,2,224,1024]{3,2,1,0:T(8,128)(2,1)} %dispatch.7), calls=%async_computation | async-start | bytes 14680064 | tf_op jit(solution)/shard_map/all_to_all | solution.py:856
  221.0 68.0 %all-gather.2.cloned.1.call-start = ((), (), s32[]{:S(2)}) async-start(), calls=%async_computation.6 | async-start | bytes 3932160 | tf_op jit(solution)/shard_map/all_gather | solution.py:1517
  222.1 16.3 %copy-start.17 = (f32[1,1,4,512]{3,1,2,0:T(1,128)}, f32[1,1,4,512]{3,1,2,0:T(1,128)S(1)}, u32[]{:S(2)}) copy-start(f32[1,1,4,512]{3,1,2,0:T(1,128)S(1)} %copy.60) | copy-start | bytes 24580
  222.1 21.4 %copy-start.33 = (s32[1,2]{1,0:T(1,128)S(1)}, s32[1,2]{1,0:T(1,128)}, u32[]{:S(2)}) copy-start(s32[1,2]{1,0:T(1,128)} %param.31) | copy-start | bytes 28
  222.1 21.6 %copy-start.31 = (bf16[512]{0:T(512)(128)(2,1)S(1)}, bf16[512]{0:T(512)(128)(2,1)}, u32[]{:S(2)}) copy-start(bf16[512]{0:T(512)(128)(2,1)} %param.24) | copy-start | bytes 3076
  222.1 21.6 %copy-start.32 = (bf16[512]{0:T(512)(128)(2,1)S(1)}, bf16[512]{0:T(512)(128)(2,1)}, u32[]{:S(2)}) copy-start(bf16[512]{0:T(512)(128)(2,1)} %param.25) | copy-start | bytes 3076
  222.1 21.6 %copy-start.26 = (s32[1536]{0:T(1024)S(1)}, s32[1536]{0:T(1024)}, u32[]{:S(2)}) copy-start(s32[1536]{0:T(1024)} %param.32) | copy-start | bytes 18436
  239.5 10.6 collective-permute-start
  239.5 10.6 collective-permute-start.1
  242.5 7.6 collective-permute-start.2
  243.8 6.3 copy-start.2
  252.7 1.1 copy-start.8
  253.8 1.1 copy-start.9
  255.0 21.7 %copy-start.35 = (bf16[512,2048]{1,0:T(8,128)(2,1)S(1)}, bf16[512,2048]{1,0:T(8,128)(2,1)}, u32[]{:S(2)}) copy-start(bf16[512,2048]{1,0:T(8,128)(2,1)} %param.21) | copy-start | bytes 6291460
  289.0 1.9 copy-start.5
  383.5 1.9 copy-start.15
  477.5 1.9 copy-start.14
  485.7 87.7 %all-to-all-start.1 = ((bf16[8,2,112,2048]{3,2,1,0:T(8,128)(2,1)}), bf16[8,2,112,2048]{3,2,1,0:T(8,128)(2,1)}, u32[]{:S(2)}, u32[]{:S(2)}) async-start(bf16[8,2,112,2048]{3,2,1,0:T(8,128)(2,1)} %dispatch.6), calls=%async_computation.1 | async-start | bytes 14680064 | tf_op jit(solution)/shard_map/all_to_all | solution.py:856
  573.4 87.7 %all-to-all-start.2 = ((bf16[8,2,112,2048]{3,2,1,0:T(8,128)(2,1)}), bf16[8,2,112,2048]{3,2,1,0:T(8,128)(2,1)}, u32[]{:S(2)}, u32[]{:S(2)}) async-start(bf16[8,2,112,2048]{3,2,1,0:T(8,128)(2,1)} %get-tuple-element.112), calls=%async_computation.2 | async-start | bytes 14680064 | tf_op jit(solution)/shard_map/all_to_all | solution.py:856
  661.1 5.0 copy-start.23
  661.1 100.7 %all-to-all-start.3 = ((bf16[8,2,112,2048]{3,2,1,0:T(8,128)(2,1)}), bf16[8,2,112,2048]{3,2,1,0:T(8,128)(2,1)}, u32[]{:S(2)}, u32[]{:S(2)}) async-start(bf16[8,2,112,2048]{3,2,1,0:T(8,128)(2,1)} %get-tuple-element.113), calls=%async_computation.3 | async-start | bytes 14680064 | tf_op jit(solution)/shard_map/all_to_all | solution.py:856
  666.4 10.7 copy-start.19
  761.8 167.0 %all-to-all-start.4 = ((bf16[8,2,224,2048]{3,2,1,0:T(8,128)(2,1)}), bf16[8,2,224,2048]{3,2,1,0:T(8,128)(2,1)}, u32[]{:S(2)}, u32[]{:S(2)}) async-start(bf16[8,2,224,2048]{3,2,1,0:T(8,128)(2,1)} %get-tuple-element.117), calls=%async_computation.4 | async-start | bytes 29360128 | tf_op jit(solution)/shard_map/all_to_all | solution.py:856
  767.4 451.8 %reduce-scatter.2.cloned.1.call-start = ((), (), s32[]{:S(2)}) async-start(), calls=%async_computation.7 | async-start | bytes 7864320 | tf_op jit(solution)/shard_map/reduce_scatter | solution.py:1614
  867.2 4.4 copy-start.24
  910.6 2.8 copy-start.3
  913.4 1.4 copy-start.10
  914.8 1.4 copy-start.12
  946.8 6.4 collective-permute-start.3
  946.8 6.4 collective-permute-start.4
  947.6 5.6 collective-permute-start.5
  1028.1 1.5 copy-start.11
  1029.6 1.4 copy-start.13
  1048.0 15.0 %copy-start.20 = (bf16[768,2048]{1,0:T(8,128)(2,1)S(1)}, bf16[768,2048]{1,0:T(8,128)(2,1)}, u32[]{:S(2)}) copy-start(bf16[768,2048]{1,0:T(8,128)(2,1)} %get-tuple-element.150) | copy-start | bytes 9437188
  1048.0 15.0 %copy-start.25 = (bf16[1536,512]{1,0:T(8,128)(2,1)S(1)}, bf16[1536,512]{1,0:T(8,128)(2,1)}, u32[]{:S(2)}) copy-start(bf16[1536,512]{1,0:T(8,128)(2,1)} %get-tuple-element.97) | copy-start | bytes 4718596
  1063.0 1.9 copy-start.34
  1206.8 2.9 copy-start.6
  1209.8 1.6 copy-start.16
  1211.4 7.2 copy-start.28
  1219.2 5.4 copy-start.21
  1219.2 6.6 copy-start.1
  (1 other events, 1.1 us)
Sparse Core Ops, SparseCore 0:
  224.0 64.9 all-gather.1
  946.8 107.4 reduce-scatter.1
